TPU v7x, 512 devices: a whole 4x4x16 slice. The times are simulated.
512 devices in a mesh: node: 128 (over y, z, core), col: 4 (over x).
Axes of the slice: x: 4, y: 4, z: 16, core: 2. Of those that a mesh axis runs over, the one named last changes fastest.
Arguments:
- features: bfloat16 [131072, 128], P('node', 'col'), may hold values from -6 to 6
- local_tiles: bfloat16 [1024, 128, 128], P('node'), may hold values from -0.125 to 0.125
- hub_tiles: bfloat16 [1024, 2, 128, 128], P('node'), may hold values from -0.125 to 0.125
- hub_ref: int32 [1024, 2], P('node'), may hold values from 0 to 127
- hub_list: int32 [128], P('node'), may hold values from 0 to 7
- send_list: int32 [128, 128], P('node'), may hold values from 0 to 7
- stripe_tiles: bfloat16 [16384, 128, 128], P('node'), may hold values from -0.125 to 0.125
- stripe_slot: int32 [128, 128], P('node'), may hold values from 0 to 127, as said below
- stripe_target: int32 [128, 128], P('node'), may hold values from 0 to 7
- stripe_live: int32 [128], P('node'), may hold values from 96 to 128, as said below
- weight: bfloat16 [128, 128], replicated, may hold values from -0.5 to 0.5
Outputs:
- layer_out: bfloat16 [131072, 128], P('node', 'col')
Inputs may be any that keep to these rules, and one draw needn't show every extreme that they name: `stripe_slot`: each row names every node device exactly once. `stripe_live`: equal to 128 on at least one node device.
All inputs are finite; a program needn't handle non-finite values.
Results may differ from a plain program's by a relative error of at most 0.0049.
Values may be sent and summed in bfloat16 or wider, within the bound.
No kernel may reach another device: no remote copies, remote signals or barrier semaphores. Data moves between devices by JAX's collectives and lax.ppermute only.
A program may use at most 64 MiB of HBM per device.

v0:
```python
import jax
import jax.numpy as jnp
from jax import lax
from jax.sharding import PartitionSpec as P


def local(
    features,
    local_tiles,
    hub_tiles,
    hub_ref,
    hub_list,
    send_list,
    stripe_tiles,
    stripe_slot,
    stripe_target,
    stripe_live,
    weight,
):
    row_blocks = local_tiles.shape[0]
    tile_size = local_tiles.shape[1]
    col_width = features.shape[1]
    capacity = stripe_tiles.shape[0]
    blocks = features.reshape(row_blocks, tile_size, col_width)
    local_sum = jnp.einsum("btu,buf->btf", local_tiles, blocks, preferred_element_type=jnp.float32)
    own_hub = blocks[hub_list]
    hub_blocks = lax.all_gather(own_hub, "node", axis=0, tiled=True)
    picked = hub_blocks[hub_ref]
    summed = local_sum + jnp.einsum(
        "bjtu,bjuf->btf", hub_tiles, picked, preferred_element_type=jnp.float32
    )
    outgoing = blocks[send_list[0]]
    received = lax.all_to_all(outgoing, "node", split_axis=0, concat_axis=0, tiled=True)
    taken = received[stripe_slot[0]]
    prods = jnp.einsum("ctu,cuf->ctf", stripe_tiles, taken, preferred_element_type=jnp.float32)
    live = jnp.arange(capacity, dtype=jnp.int32) < stripe_live[0]
    onehot = (
        (stripe_target[0][None, :] == jnp.arange(row_blocks, dtype=jnp.int32)[:, None])
        & live[None, :]
    ).astype(jnp.float32)
    stripe_sum = jnp.dot(
        onehot, prods.reshape(capacity, tile_size * col_width), precision=lax.Precision.HIGHEST
    )
    summed = summed + stripe_sum.reshape(row_blocks, tile_size, col_width)
    aggregated = summed.astype(jnp.bfloat16).reshape(row_blocks * tile_size, col_width)
    column = lax.axis_index("col")
    full_rows = lax.all_gather(aggregated, "col", axis=1, tiled=True)
    weight_cols = lax.dynamic_slice_in_dim(weight, column * col_width, col_width, 1)
    result = jnp.dot(full_rows, weight_cols, preferred_element_type=jnp.float32)
    return result.astype(jnp.bfloat16)


def solution(mesh):
    in_specs = (
        P("node", "col"),
        P("node", None, None),
        P("node", None, None, None),
        P("node", None),
        P("node"),
        P("node", None),
        P("node", None, None),
        P("node", None),
        P("node", None),
        P("node"),
        P(),
    )
    out_specs = P("node", "col")
    return jax.shard_map(local, mesh=mesh, in_specs=in_specs, out_specs=out_specs, check_vma=False)
```

profile of v0, /device:TPU:1, one launch (start us, length us, event | category | flops | bytes accessed | tf_op | source)
XLA Modules:
  0.0 196.8 jit_solution(7327114405169538252)
XLA Ops:
  6.5 0.0 copy-start
  6.5 0.9 copy_bitcast_fusion.1
  7.4 0.7 fusion.12
  8.1 0.0 copy-start.1
  8.1 0.0 copy-start.4
  8.1 0.0 copy-start.6
  8.1 0.0 copy-start.2
  8.2 1.7 gather_fusion.1
  9.8 20.6 %all-to-all-start = ((bf16[128,128,32]{1,2,0:T(8,128)(2,1)}), bf16[128,128,32]{1,2,0:T(8,128)(2,1)S(1)}, u32[]{:S(2)}, u32[]{:S(2)}) async-start(bf16[128,128,32]{1,2,0:T(8,128)(2,1)} %gather_fusion.1), calls=%async_computation | async-start | bytes 2097152 | tf_op jit(solution)/shard_map/all_to_all | solution.py:33
  30.4 0.0 all-gather.2.cloned.1.call-start
  31.1 0.0 copy-done.1
  31.2 0.6 copy.30
  31.8 0.0 all-gather.2.cloned.1.call-update
  31.8 0.0 copy-done.4
  31.8 0.1 copy.31
  31.9 0.1 reshape.98
  32.7 0.0 copy-done.6
  32.7 0.0 copy-done.2
  32.7 0.2 fusion.15
  32.9 136.4 %all-gather.2.cloned.1.call-done = bf16[128,128,32]{1,2,0:T(8,128)(2,1)} async-done(((bf16[1,128,32]{1,2,0:T(8,128)(2,1)}), bf16[128,128,32]{1,2,0:T(8,128)(2,1)}) %all-gather.2.cloned.1.call-update) | async-done | bytes 1048592 | tf_op jit(solution)/shard_map/all_gather | solution.py:27
  169.4 1.8 gather_fusion
  171.2 0.0 all-to-all-done
  171.2 0.8 gather_fusion.2
  171.9 0.0 copy-start.5
  172.0 0.0 copy-start.3
  172.0 4.5 %convolution_bitcast_fusion = f32[128,32,128]{0,1,2:T(8,128)S(1)} fusion(bf16[128,128,32]{1,2,0:T(8,128)(2,1)S(1)} %gather_fusion.2, bf16[128,128,128]{2,1,0:T(8,128)(2,1)} %param.17), kind=kOutput, calls=%fused_computation.5 | convolution fusion | flops 134217728 | bytes 7340032 | tf_op jit(solution)/shard_map/ctu,cuf->ctf/dot_general | solution.py:35
  176.4 0.0 copy-done.5
  176.4 2.0 %fusion = f32[8,128,32]{1,0,2:T(8,128)S(1)} fusion(f32[128,32,128]{0,1,2:T(8,128)S(1)} %convolution_bitcast_fusion, s32[128]{0:T(128)S(1)} %bitcast.64, pred[128]{0:T(512)(128)(4,1)S(1)} %iota_compare_fusion.1), kind=kOutput, calls=%fused_computation.3 | convolution fusion | flops 50333696 | bytes 2228864 | tf_op jit(solution)/shard_map/dot_general | solution.py:41
  178.4 0.0 copy-done
  178.4 0.3 fusion.5
  178.7 10.3 %all_gather.7 = bf16[1024,128]{0,1:T(8,128)(2,1)S(1)} all-gather(bf16[1024,32]{0,1:T(8,128)(2,1)S(1)} %bitcast.62), channel_id=1, replica_groups=mesh['node'=128,'col'=4] {'col'}, dimensions={1}, use_global_device_ids=true | all-gather | bytes 327680 | tf_op jit(solution)/shard_map/all_gather | solution.py:47
  189.0 0.0 copy-done.3
  189.0 0.9 convolution_convert_fusion
  (9 shorter events, 0.1 us)
Async XLA Ops:
  6.5 171.9 %copy-start = (bf16[8,2,128,128]{3,2,1,0:T(8,128)(2,1)S(1)}, bf16[8,2,128,128]{3,2,1,0:T(8,128)(2,1)}, u32[]{:S(2)}) copy-start(bf16[8,2,128,128]{3,2,1,0:T(8,128)(2,1)} %param.13) | copy-start | bytes 1572868
  8.1 23.0 %copy-start.1 = (bf16[1024,32]{0,1:T(8,128)(2,1)S(1)}, bf16[1024,32]{0,1:T(8,128)(2,1)}, u32[]{:S(2)}) copy-start(bf16[1024,32]{0,1:T(8,128)(2,1)} %param.11) | copy-start | bytes 196612
  8.1 23.7 %copy-start.4 = (s32[8,2]{0,1:T(2,128)S(1)}, s32[8,2]{0,1:T(2,128)}, u32[]{:S(2)}) copy-start(s32[8,2]{0,1:T(2,128)} %param.14) | copy-start | bytes 196
  8.1 24.5 %copy-start.6 = (s32[1,128]{1,0:T(1,128)S(1)}, s32[1,128]{1,0:T(1,128)}, u32[]{:S(2)}) copy-start(s32[1,128]{1,0:T(1,128)} %param.18) | copy-start | bytes 1540
  8.1 24.5 %copy-start.2 = (bf16[8,128,128]{2,1,0:T(8,128)(2,1)S(1)}, bf16[8,128,128]{2,1,0:T(8,128)(2,1)}, u32[]{:S(2)}) copy-start(bf16[8,128,128]{2,1,0:T(8,128)(2,1)} %param.12) | copy-start | bytes 786436
  9.8 161.3 %all-to-all-start = ((bf16[128,128,32]{1,2,0:T(8,128)(2,1)}), bf16[128,128,32]{1,2,0:T(8,128)(2,1)S(1)}, u32[]{:S(2)}, u32[]{:S(2)}) async-start(bf16[128,128,32]{1,2,0:T(8,128)(2,1)} %gather_fusion.1), calls=%async_computation | async-start | bytes 2097152 | tf_op jit(solution)/shard_map/all_to_all | solution.py:33
  30.4 139.0 %all-gather.2.cloned.1.call-start = ((), (), s32[]{:S(2)}) async-start(), calls=%async_computation.1 | async-start | bytes 1056768 | tf_op jit(solution)/shard_map/all_gather | solution.py:27
  171.9 4.5 %copy-start.5 = (s32[1,128]{1,0:T(1,128)S(1)}, s32[1,128]{1,0:T(1,128)}, u32[]{:S(2)}) copy-start(s32[1,128]{1,0:T(1,128)} %param.19) | copy-start | bytes 1540
  172.0 17.1 %copy-start.3 = (bf16[128,128]{1,0:T(8,128)(2,1)S(1)}, bf16[128,128]{1,0:T(8,128)(2,1)}, u32[]{:S(2)}) copy-start(bf16[128,128]{1,0:T(8,128)(2,1)} %param.21) | copy-start | bytes 98308
Sparse Core Ops, SparseCore 0:
  34.2 135.1 all-gather.1
where the time goes:
time: 198 us; the launch traced here: 197 us
  waiting for transfers between devices  136 us (69%)
  starting transfers between devices  20.6 us (10%)
  between operations  14.9 us (8%)
  blocking collectives  10.3 us (5%)
  matrix products  7.88 us (4%)
  local copies, waits for them, and re-layouts  5.98 us (3%)
    all_gather x1, waiting for transfers between devices, local(): hub_blocks = lax.all_gather(own_hub, 'node', axis=0, tiled=True)  136 us
    all_to_all x1, starting transfers between devices, local(): lax.all_to_all(outgoing, 'node', split_axis=0, concat_axis=0, tiled=True)  20.6 us
    all_gather x1, blocking collectives, local(): full_rows = lax.all_gather(aggregated, 'col', axis=1, tiled=True)  10.3 us
    dot_general x1, matrix products, local(): jnp.einsum('ctu,cuf->ctf', stripe_tiles, taken, preferred_element_type=jn...  4.48 us
  transfers between devices with their start and end apart: 2, of which 1 were waited for; matrix products, arithmetic and copies ran while one was open for 1% of the time, Pallas kernels for 0%

commit v1 on v0

v1 whole, which is shorter than its diff:
```python
import functools

import jax
import jax.numpy as jnp
from jax import lax
from jax.experimental import pallas as pl
from jax.experimental.pallas import tpu as pltpu
from jax.sharding import Mesh, PartitionSpec as P

Y, H, L, C, COL = 4, 4, 4, 2, 4
ROWB, TILE, W = 8, 128, 32
NEAR = Y * L * C
CAP = 128
BLOCKS = ROWB * W
PAY = BLOCKS + 16
CHUNKS = 8
NT = (((1,), (1,)), ((), ()))
VMEM = pl.BlockSpec(memory_space=pltpu.VMEM)
SMEM = pl.BlockSpec(memory_space=pltpu.SMEM)
ANY = pl.BlockSpec(memory_space=pl.ANY)


def rows_of(start):
    return pl.ds(pl.multiple_of(start, 16), W)


def pack_kernel(hub_list, feat, send, out):
    for b in range(ROWB):
        out[b * W : (b + 1) * W, :] = feat[:, b * TILE : (b + 1) * TILE]
    row = lax.broadcasted_iota(jnp.int32, (16, TILE), 0)
    sends = jnp.broadcast_to(send[...], (16, TILE))
    meta = jnp.where(row == 0, sends, hub_list[0])
    out[BLOCKS:PAY, :] = meta.astype(jnp.float32).astype(jnp.bfloat16)


def select_kernel(gathered, out, hubs, index_vmem, index, sem):
    for h in range(H):
        meta = gathered[h * PAY + BLOCKS : (h + 1) * PAY, :].astype(jnp.float32)
        index_vmem[h * 8 : h * 8 + 8, :] = meta[:8].astype(jnp.int32)
    copy = pltpu.make_async_copy(index_vmem, index, sem)
    copy.start()
    copy.wait()
    cube = lax.axis_index("h")
    for h in range(H):
        hubs[h * W : (h + 1) * W, :] = gathered[rows_of(h * PAY + index[h * 8 + 1, 0] * W), :]
    for m in range(NEAR):
        reader = (m // (L * C)) * (H * L * C) + cube * (L * C) + m % (L * C)
        for h in range(H):
            block = index[h * 8, reader]
            at = (m * H + h) * W
            out[at : at + W, :] = gathered[rows_of(h * PAY + block * W), :]


def base_kernel(hub_ref, feat, local_tiles, hub_tiles, hubs_own, hubs_other, out):
    core = lax.axis_index("c")
    for b in range(ROWB):
        total = lax.dot_general(
            feat[:, b * TILE : (b + 1) * TILE], local_tiles[b], NT, preferred_element_type=jnp.float32
        )
        for j in range(2):
            hub = hub_ref[b, j]
            y = lax.shift_right_logical(hub, 5)
            h = lax.shift_right_logical(hub, 3) & 3
            l = lax.shift_right_logical(hub, 1) & 3
            at = rows_of(((y * L + l) * H + h) * W)
            block = jnp.where((hub & 1) == core, hubs_own[at, :], hubs_other[at, :])
            total += lax.dot_general(block, hub_tiles[b, j], NT, preferred_element_type=jnp.float32)
        out[b * W : (b + 1) * W, :] = total


def stripe_kernel(slot, target, live, received, base, tiles_hbm, out, tiles, acc, sems):
    each = CAP // CHUNKS
    copies = []
    for k in range(CHUNKS):
        part = pl.ds(k * each, each)
        copies.append(pltpu.make_async_copy(tiles_hbm.at[part], tiles.at[part], sems.at[k]))
        copies[-1].start()
    acc[0:BLOCKS, :] = base[...]
    acc[BLOCKS:, :] = jnp.zeros((W, TILE), jnp.float32)
    count = live[0]
    for k in range(CHUNKS):
        copies[k].wait()
        for s in range(k * each, (k + 1) * each):
            q = slot[0, s]
            y = lax.shift_right_logical(q, 5)
            h = lax.shift_right_logical(q, 3) & 3
            near = y * (L * C) + (q & 7)
            block = received[rows_of((near * H + h) * W), :]
            prod = lax.dot_general(block, tiles[s], NT, preferred_element_type=jnp.float32)
            row = jnp.where(s < count, target[0, s], ROWB)
            acc[rows_of(row * W), :] += prod
    for b in range(ROWB):
        agg = acc[b * W : (b + 1) * W, :].astype(jnp.bfloat16)
        for k in range(COL):
            out[k * W : (k + 1) * W, b * TILE : (b + 1) * TILE] = agg


def local(
    features,
    local_tiles,
    hub_tiles,
    hub_ref,
    hub_list,
    send_list,
    stripe_tiles,
    stripe_slot,
    stripe_target,
    stripe_live,
    weight,
):
    bf16, f32 = jnp.bfloat16, jnp.float32
    params = pltpu.CompilerParams(vmem_limit_bytes=32 * 1024 * 1024)
    feat = features.T
    payload = pl.pallas_call(
        pack_kernel,
        out_shape=jax.ShapeDtypeStruct((PAY, TILE), bf16),
        in_specs=[SMEM, VMEM, VMEM],
        out_specs=VMEM,
        compiler_params=params,
        name="pack",
    )(hub_list, feat, send_list)
    gathered = lax.all_gather(payload, "h", axis=0, tiled=True)
    outgoing, hubs = pl.pallas_call(
        select_kernel,
        out_shape=(
            jax.ShapeDtypeStruct((NEAR * H * W, TILE), bf16),
            jax.ShapeDtypeStruct((H * W, TILE), bf16),
        ),
        in_specs=[VMEM],
        out_specs=(VMEM, VMEM),
        scratch_shapes=[
            pltpu.VMEM((H * 8, TILE), jnp.int32),
            pltpu.SMEM((H * 8, TILE), jnp.int32),
            pltpu.SemaphoreType.DMA,
        ],
        compiler_params=params,
        name="select",
    )(gathered)
    hubs_l = lax.all_gather(hubs, "l", axis=0, tiled=True)
    hubs_l, outgoing = lax.optimization_barrier((hubs_l, outgoing))
    received = lax.all_to_all(outgoing, ("y", "l", "c"), split_axis=0, concat_axis=0, tiled=True)
    hubs_own = lax.all_gather(hubs_l, "y", axis=0, tiled=True)
    hubs_other = lax.ppermute(hubs_own, "c", [(0, 1), (1, 0)])
    base = pl.pallas_call(
        base_kernel,
        out_shape=jax.ShapeDtypeStruct((BLOCKS, TILE), f32),
        in_specs=[SMEM, VMEM, VMEM, VMEM, VMEM, VMEM],
        out_specs=VMEM,
        compiler_params=params,
        cost_estimate=pl.CostEstimate(flops=25_000_000, bytes_accessed=2_000_000, transcendentals=0),
        name="base",
    )(hub_ref, feat, local_tiles, hub_tiles, hubs_own, hubs_other)
    aggregated = pl.pallas_call(
        stripe_kernel,
        out_shape=jax.ShapeDtypeStruct((COL * W, ROWB * TILE), bf16),
        in_specs=[SMEM, SMEM, SMEM, VMEM, VMEM, ANY],
        out_specs=VMEM,
        scratch_shapes=[
            pltpu.VMEM((CAP, TILE, TILE), bf16),
            pltpu.VMEM((BLOCKS + W, TILE), f32),
            pltpu.SemaphoreType.DMA((CHUNKS,)),
        ],
        compiler_params=params,
        name="stripes",
    )(stripe_slot, stripe_target, stripe_live, received, base, stripe_tiles)
    full = lax.all_to_all(aggregated, "x", split_axis=0, concat_axis=0, tiled=True)
    weight_cols = lax.dynamic_slice_in_dim(weight, lax.axis_index("x") * W, W, 1)
    result = jnp.dot(weight_cols.T, full, preferred_element_type=f32)
    return result.astype(bf16).T


def solution(mesh):
    split = Mesh(mesh.devices.reshape(Y, H, L, C, COL), ("y", "h", "l", "c", "x"))
    node = ("y", "h", "l", "c")
    in_specs = (
        P(node, "x"),
        P(node, None, None),
        P(node, None, None, None),
        P(node, None),
        P(node),
        P(node, None),
        P(node, None, None),
        P(node, None),
        P(node, None),
        P(node),
        P(),
    )
    return jax.shard_map(local, mesh=split, in_specs=in_specs, out_specs=P(node, "x"), check_vma=False)
```

time: 198 us -> 98.4 us (0.50)
  waiting for transfers between devices: 136 us -> 7.82 us
  blocking collectives: 10.3 us -> 52.2 us
  between operations: 14.9 us -> 1.39 us
  Pallas kernels: 0 us -> 8.02 us
  matrix products: 7.88 us -> 0.91 us
    all_gather x1 -> x0, waiting for transfers between devices: 136 us -> none  [local(): hub_blocks = lax.all_gather(own_hub, 'node', axis=0, tiled=True)]
    all_gather x1 -> x3, blocking collectives: 10.3 us -> 52.2 us  [the longest x1 25.3 us: local(): gathered = lax.all_gather(payload, 'h', axis=0, tiled=True)]
    pallas_call x0 -> x4, Pallas kernels: none -> 8.02 us  [the longest x1 4.81 us: local(): pl.pallas_call(stripe_kernel, out_shape=jax.ShapeDtypeStruct((COL * W, RO...]
    all_to_all x1 -> x2, waiting for transfers between devices: 0.01 us -> 7.71 us  [the longest x1 5.86 us: local(): lax.all_to_all(aggregated, 'x', split_axis=0, concat_axis=0, tiled=True)]
    unnamed x15 -> x19, local copies, waits for them, and re-layouts: 0.05 us -> 7.28 us
    dot_general x5 -> x1, matrix products: 7.88 us -> 0.91 us  [local(): result = jnp.dot(weight_cols.T, full, preferred_element_type=f32)]
    gather x5 -> x0, local copies, waits for them, and re-layouts: 4.84 us -> none  [the longest x1 1.8 us: local(): picked = hub_blocks[hub_ref]]
    all_to_all x1 -> x2, starting transfers between devices: 20.6 us -> 16.1 us  [the longest x1 12 us: local(): lax.all_to_all(outgoing, ('y', 'l', 'c'), split_axis=0, concat_axis=0, ti...]
  transfers between devices with their start and end apart: 2 -> 3, of which waited for: 1 -> 3; matrix products, arithmetic and copies ran while one was open for 1% -> 1% of each run, Pallas kernels for 0% -> 1%
where the time goes in v1:
time: 98.4 us; the launch traced here: 97.8 us
  blocking collectives  52.2 us (53%)
  starting transfers between devices  20.2 us (21%)
  Pallas kernels  8.02 us (8%)
  waiting for transfers between devices  7.82 us (8%)
  local copies, waits for them, and re-layouts  7.28 us (7%)
  between operations  1.39 us (1%)
    all_gather x1, blocking collectives, local(): gathered = lax.all_gather(payload, 'h', axis=0, tiled=True)  25.3 us
    all_gather x1, blocking collectives, local(): hubs_own = lax.all_gather(hubs_l, 'y', axis=0, tiled=True)  16.4 us
    all_to_all x1, starting transfers between devices, local(): lax.all_to_all(outgoing, ('y', 'l', 'c'), split_axis=0, concat_axis=0, ti...  12 us
    all_gather x1, blocking collectives, local(): hubs_l = lax.all_gather(hubs, 'l', axis=0, tiled=True)  10.5 us
    unnamed x19, local copies, waits for them, and re-layouts  7.28 us
    all_to_all x1, waiting for transfers between devices, local(): lax.all_to_all(aggregated, 'x', split_axis=0, concat_axis=0, tiled=True)  5.86 us
    pallas_call x1, Pallas kernels, local(): pl.pallas_call(stripe_kernel, out_shape=jax.ShapeDtypeStruct((COL * W, RO...  4.81 us
    ppermute x1, starting transfers between devices, local(): hubs_other = lax.ppermute(hubs_own, 'c', [(0, 1), (1, 0)])  4.13 us
  transfers between devices with their start and end apart: 3, of which 3 were waited for; matrix products, arithmetic and copies ran while one was open for 1% of the time, Pallas kernels for 1%

profile of v1, /device:TPU:1, one launch (start us, length us, event | category | flops | bytes accessed | tf_op | source)
XLA Modules:
  0.0 97.8 jit_solution(3489101622256342599)
XLA Ops:
  0.0 0.0 copy-start
  0.0 0.0 copy-start.7
  0.0 0.0 copy-start.8
  0.7 0.0 copy-start.3
  0.7 0.8 copy-done.3
  1.5 0.0 copy-start.6
  1.5 0.7 copy-done.6
  2.2 25.3 %all_gather.9.gathered = bf16[1088,128]{1,0:T(8,128)(2,1)S(1)} all-gather(bf16[272,128]{1,0:T(8,128)(2,1)S(1)} %pack.1), channel_id=1, replica_groups=mesh['y'=4,'h'=4,'l'=4,'c'=2,'x'=4] {'h'}, dimensions={0}, use_global_device_ids=true | all-gather | bytes 348160 | tf_op jit(solution)/shard_map/all_gather | solution.py:122
  27.5 2.1 %select.1 = (bf16[4096,128]{1,0:T(8,128)(2,1)}, bf16[128,128]{1,0:T(8,128)(2,1)S(1)}) custom-call(bf16[1088,128]{1,0:T(8,128)(2,1)S(1)} %all_gather.9.gathered), custom_call_target="tpu_custom_call" | custom-call | tf_op jit(solution)/shard_map/select/pallas_call | solution.py:123
  29.6 10.5 %all_gather.10 = bf16[512,128]{1,0:T(8,128)(2,1)S(1)} all-gather(bf16[128,128]{1,0:T(8,128)(2,1)S(1)} %get-tuple-element.9), channel_id=1, replica_groups=mesh['y'=4,'h'=4,'l'=4,'c'=2,'x'=4] {'l'}, dimensions={0}, use_global_device_ids=true | all-gather | bytes 163840 | tf_op jit(solution)/shard_map/all_gather | solution.py:139
  40.0 12.0 %all-to-all-start = ((bf16[32,128,128]{2,1,0:T(8,128)(2,1)}), bf16[32,128,128]{2,1,0:T(8,128)(2,1)S(1)}, u32[]{:S(2)}, u32[]{:S(2)}) async-start(bf16[32,128,128]{2,1,0:T(8,128)(2,1)} %bitcast.1), calls=%async_computation | async-start | bytes 2097152 | tf_op jit(solution)/shard_map/all_to_all | solution.py:141
  52.1 16.4 %all_gather.11.hubs_own = bf16[2048,128]{1,0:T(8,128)(2,1)S(1)} all-gather(bf16[512,128]{1,0:T(8,128)(2,1)S(1)} %all_gather.10), channel_id=1, replica_groups=mesh['y'=4,'h'=4,'l'=4,'c'=2,'x'=4] {'y'}, dimensions={0}, use_global_device_ids=true | all-gather | bytes 655360 | tf_op jit(solution)/shard_map/all_gather | solution.py:142
  68.5 4.1 %collective-permute-start = (bf16[2048,128]{1,0:T(8,128)(2,1)S(1)}, bf16[2048,128]{1,0:T(8,128)(2,1)S(1)}, u32[]{:S(2)}, u32[]{:S(2)}) collective-permute-start(bf16[2048,128]{1,0:T(8,128)(2,1)S(1)} %all_gather.11.hubs_own), channel_id=1, source_target_pairs={{0,4},{4,0},{1,5},{5,1},{2,6},{6,2},{3,7},{7,3},{8,12},{12,8},{9,1... | collective-permute-start | bytes 1572872 | tf_op jit(solution)/shard_map/ppermute | solution.py:143
  72.6 0.8 copy.12.hub_ref
  74.1 0.1 collective-permute-done.hubs_other
  74.2 0.0 copy-start.2
  74.2 1.0 %copy-done.2 = bf16[8,2,128,128]{3,2,1,0:T(8,128)(2,1)S(1)} copy-done((bf16[8,2,128,128]{3,2,1,0:T(8,128)(2,1)S(1)}, bf16[8,2,128,128]{3,2,1,0:T(8,128)(2,1)}, u32[]{:S(2)}) %copy-start.2) | copy-done | bytes 524312
  75.2 0.0 copy-start.4
  75.2 0.8 copy-done.4
  76.0 0.0 copy-start.5
  76.0 0.9 copy-done.5
  77.0 1.1 %base.1 = f32[256,128]{1,0:T(8,128)S(1)} custom-call(s32[8,2]{1,0:T(8,128)S(1)} %copy.12.hub_ref, bf16[32,1024]{1,0:T(8,128)(2,1)S(1)} %bitcast.8, bf16[8,128,128]{2,1,0:T(8,128)(2,1)S(1)} %copy-done.5, bf16[8,2,128,128]{3,2,1,0:T(8,128)(2,1)S(1)} %copy-done.2, bf16[2048,128]{1,0:T(8,128)(2,1)S(1)} %all_gather.11.hubs_own, ...), custom_call_target="tpu_custom_call" | custom-call | flops 25000000 | bytes 2000000 | tf_op jit(solution)/shard_map/base/pallas_call | solution.py:144
  78.1 1.9 %all-to-all-done = bf16[32,128,128]{2,1,0:T(8,128)(2,1)S(1)} async-done(((bf16[32,128,128]{2,1,0:T(8,128)(2,1)}), bf16[32,128,128]{2,1,0:T(8,128)(2,1)S(1)}, u32[]{:S(2)}, u32[]{:S(2)}) %all-to-all-start) | async-done | bytes 1048608 | tf_op jit(solution)/shard_map/all_to_all | solution.py:141
  80.0 0.0 copy-done.7
  80.0 0.0 copy-done.8
  80.0 0.0 copy-start.1
  80.0 2.2 %copy-done.1 = bf16[128,128,128]{2,1,0:T(8,128)(2,1)S(1)} copy-done((bf16[128,128,128]{2,1,0:T(8,128)(2,1)S(1)}, bf16[128,128,128]{2,1,0:T(8,128)(2,1)}, u32[]{:S(2)}) %copy-start.1) | copy-done | bytes 4194328
  82.1 4.8 %stripes.1 = bf16[128,1024]{1,0:T(8,128)(2,1)} custom-call(s32[1,128]{1,0:T(1,128)S(1)} %copy-done.7, s32[1,128]{1,0:T(1,128)S(1)} %copy-done.8, s32[1]{0:T(128)S(6)} %copy.14.live, bf16[4096,128]{1,0:T(8,128)(2,1)S(1)} %bitcast.6, f32[256,128]{1,0:T(8,128)S(1)} %base.1, bf16[128,128,128]{2,1,0:T(8,128)(2,1)S(1)} %copy-done.1), custom_call_target="tpu_custom_call" | custom-call | tf_op jit(solution)/shard_map/stripes/pallas_call | solution.py:153
  87.0 4.0 %all-to-all-start.1 = ((bf16[4,32,1024]{2,1,0:T(8,128)(2,1)}), bf16[4,32,1024]{2,1,0:T(8,128)(2,1)S(1)}, u32[]{:S(2)}, u32[]{:S(2)}) async-start(bf16[4,32,1024]{2,1,0:T(8,128)(2,1)} %bitcast.3), calls=%async_computation.1 | async-start | bytes 524288 | tf_op jit(solution)/shard_map/all_to_all | solution.py:166
  91.0 5.9 %all-to-all-done.1 = bf16[4,32,1024]{2,1,0:T(8,128)(2,1)S(1)} async-done(((bf16[4,32,1024]{2,1,0:T(8,128)(2,1)}), bf16[4,32,1024]{2,1,0:T(8,128)(2,1)S(1)}, u32[]{:S(2)}, u32[]{:S(2)}) %all-to-all-start.1) | async-done | bytes 262176 | tf_op jit(solution)/shard_map/all_to_all | solution.py:166
  96.9 0.0 copy-done
  96.9 0.9 convolution_convert_fusion
  (1 shorter events, 0.0 us)
Async XLA Ops:
  0.0 96.9 %copy-start = (bf16[128,128]{1,0:T(8,128)(2,1)S(1)}, bf16[128,128]{1,0:T(8,128)(2,1)}, u32[]{:S(2)}) copy-start(bf16[128,128]{1,0:T(8,128)(2,1)} %param.21) | copy-start | bytes 98308
  0.0 80.0 %copy-start.7 = (s32[1,128]{1,0:T(1,128)S(1)}, s32[1,128]{1,0:T(1,128)}, u32[]{:S(2)}) copy-start(s32[1,128]{1,0:T(1,128)} %slot.1) | copy-start | bytes 1540
  0.0 80.0 %copy-start.8 = (s32[1,128]{1,0:T(1,128)S(1)}, s32[1,128]{1,0:T(1,128)}, u32[]{:S(2)}) copy-start(s32[1,128]{1,0:T(1,128)} %target.1) | copy-start | bytes 1540
  0.7 0.8 copy-start.3
  1.5 0.7 copy-start.6
  40.0 39.9 %all-to-all-start = ((bf16[32,128,128]{2,1,0:T(8,128)(2,1)}), bf16[32,128,128]{2,1,0:T(8,128)(2,1)S(1)}, u32[]{:S(2)}, u32[]{:S(2)}) async-start(bf16[32,128,128]{2,1,0:T(8,128)(2,1)} %bitcast.1), calls=%async_computation | async-start | bytes 2097152 | tf_op jit(solution)/shard_map/all_to_all | solution.py:141
  68.5 5.7 %collective-permute-start = (bf16[2048,128]{1,0:T(8,128)(2,1)S(1)}, bf16[2048,128]{1,0:T(8,128)(2,1)S(1)}, u32[]{:S(2)}, u32[]{:S(2)}) collective-permute-start(bf16[2048,128]{1,0:T(8,128)(2,1)S(1)} %all_gather.11.hubs_own), channel_id=1, source_target_pairs={{0,4},{4,0},{1,5},{5,1},{2,6},{6,2},{3,7},{7,3},{8,12},{12,8},{9,1... | collective-permute-start | bytes 1572872 | tf_op jit(solution)/shard_map/ppermute | solution.py:143
  74.2 1.0 %copy-start.2 = (bf16[8,2,128,128]{3,2,1,0:T(8,128)(2,1)S(1)}, bf16[8,2,128,128]{3,2,1,0:T(8,128)(2,1)}, u32[]{:S(2)}) copy-start(bf16[8,2,128,128]{3,2,1,0:T(8,128)(2,1)} %hub_tiles.1) | copy-start | bytes 1572868
  75.2 0.8 copy-start.4
  76.0 0.9 copy-start.5
  80.0 2.2 %copy-start.1 = (bf16[128,128,128]{2,1,0:T(8,128)(2,1)S(1)}, bf16[128,128,128]{2,1,0:T(8,128)(2,1)}, u32[]{:S(2)}) copy-start(bf16[128,128,128]{2,1,0:T(8,128)(2,1)} %tiles_hbm.1) | copy-start | bytes 12582916
  87.0 9.9 %all-to-all-start.1 = ((bf16[4,32,1024]{2,1,0:T(8,128)(2,1)}), bf16[4,32,1024]{2,1,0:T(8,128)(2,1)S(1)}, u32[]{:S(2)}, u32[]{:S(2)}) async-start(bf16[4,32,1024]{2,1,0:T(8,128)(2,1)} %bitcast.3), calls=%async_computation.1 | async-start | bytes 524288 | tf_op jit(solution)/shard_map/all_to_all | solution.py:166

commit v2 on v1

v2 whole, which is shorter than its diff:
```python
import jax
import jax.numpy as jnp
from jax import lax
from jax.experimental import pallas as pl
from jax.experimental.pallas import tpu as pltpu
from jax.sharding import Mesh, PartitionSpec as P

Y, H, L, C, COL = 4, 8, 2, 2, 4
ROWB, TILE, W = 8, 128, 32
NEAR = Y * L * C
CAP = 128
EARLY = 40
PARTS = 4
BLOCKS = ROWB * W
META = BLOCKS + W
PAY = META + 16
SENT = 2 * H * W
NT = (((1,), (1,)), ((), ()))
VMEM = pl.BlockSpec(memory_space=pltpu.VMEM)
SMEM = pl.BlockSpec(memory_space=pltpu.SMEM)
ANY = pl.BlockSpec(memory_space=pl.ANY)


def rows_of(start):
    return pl.ds(pl.multiple_of(start, 16), W)


def in_hbm(array):
    return pltpu.with_memory_space_constraint(array, pltpu.HBM)


def in_vmem(array):
    return pltpu.with_memory_space_constraint(array, pltpu.VMEM)


def pack_kernel(hub_list, feat, send, out):
    for b in range(ROWB):
        out[b * W : (b + 1) * W, :] = feat[:, b * TILE : (b + 1) * TILE]
    sends = jnp.broadcast_to(send[...], (16, TILE))
    out[META:PAY, :] = sends.astype(jnp.float32).astype(jnp.bfloat16)
    out[BLOCKS:META, :] = out[rows_of(hub_list[0] * W), :]


def select_kernel(gathered, out, index_vmem, index, buffer, sem, sems):
    for h in range(H):
        meta = gathered[h * PAY + META : (h + 1) * PAY, :].astype(jnp.float32)
        index_vmem[h * 8 : h * 8 + 8, :] = meta[:8].astype(jnp.int32)
    copy = pltpu.make_async_copy(index_vmem, index, sem)
    copy.start()
    for m in range(NEAR):
        for h in range(H):
            at = (H + h) * W
            buffer[m, at : at + W, :] = gathered[h * PAY + BLOCKS : h * PAY + META, :]
    copy.wait()
    pair = lax.axis_index("h")
    copies = []
    for m in range(NEAR):
        reader = (m // (L * C)) * (H * L * C) + pair * (L * C) + m % (L * C)
        for h in range(H):
            block = index[h * 8, reader]
            buffer[m, h * W : (h + 1) * W, :] = gathered[rows_of(h * PAY + block * W), :]
        copies.append(pltpu.make_async_copy(buffer.at[m], out.at[m], sems.at[m]))
        copies[-1].start()
    for copy in copies:
        copy.wait()


def fetch_kernel(feat, local_tiles, tiles_hbm, out, tiles, sem):
    copy = pltpu.make_async_copy(tiles_hbm.at[pl.ds(0, EARLY)], tiles, sem)
    copy.start()
    for b in range(ROWB):
        out[b * W : (b + 1) * W, :] = lax.dot_general(
            feat[:, b * TILE : (b + 1) * TILE], local_tiles[b], NT, preferred_element_type=jnp.float32
        )
    copy.wait()


def stripe_kernel(
    hub_ref, slot, target, live, received, base, early, hub_hbm, tiles_hbm, out, hub_tiles, late, acc, hub_sem, sems
):
    each = (CAP - EARLY) // PARTS
    hub_copy = pltpu.make_async_copy(hub_hbm, hub_tiles, hub_sem)
    hub_copy.start()
    copies = []
    for k in range(PARTS):
        source = tiles_hbm.at[pl.ds(EARLY + k * each, each)]
        copies.append(pltpu.make_async_copy(source, late.at[pl.ds(k * each, each)], sems.at[k]))
        copies[-1].start()

    def place(node):
        near = lax.shift_right_logical(node, 5) * (L * C) + (node & 3)
        return near * SENT, (lax.shift_right_logical(node, 2) & 7) * W

    def product(tile, start):
        return lax.dot_general(tile, received[rows_of(start), :], NT, preferred_element_type=jnp.float32)

    for b in range(ROWB + 1):
        acc[b] = jnp.zeros((TILE, W), jnp.float32)
    count = live[0]
    for s in range(CAP):
        if s == EARLY:
            hub_copy.wait()
            for b in range(ROWB):
                total = acc[b]
                for j in range(2):
                    near, at = place(hub_ref[b, j])
                    total += product(hub_tiles[b, j], near + H * W + at)
                acc[b] = total
        if s >= EARLY and (s - EARLY) % each == 0:
            copies[(s - EARLY) // each].wait()
        tile = early[s] if s < EARLY else late[s - EARLY]
        near, at = place(slot[0, s])
        row = jnp.where(s < count, target[0, s], ROWB)
        acc[row] += product(tile, near + at)
    for b in range(ROWB):
        agg = (acc[b].T + base[b * W : (b + 1) * W, :]).astype(jnp.bfloat16)
        for k in range(COL):
            out[k * W : (k + 1) * W, b * TILE : (b + 1) * TILE] = agg


def local(
    features,
    local_tiles,
    hub_tiles,
    hub_ref,
    hub_list,
    send_list,
    stripe_tiles,
    stripe_slot,
    stripe_target,
    stripe_live,
    weight,
):
    bf16, f32 = jnp.bfloat16, jnp.float32
    params = pltpu.CompilerParams(vmem_limit_bytes=16 * 1024 * 1024)
    feat = features.T
    payload = pl.pallas_call(
        pack_kernel,
        out_shape=jax.ShapeDtypeStruct((PAY, TILE), bf16),
        in_specs=[SMEM, VMEM, VMEM],
        out_specs=VMEM,
        compiler_params=params,
        name="pack",
    )(hub_list, in_hbm(feat), in_hbm(send_list))
    gathered = lax.all_gather(payload, "h", axis=0, tiled=True)
    outgoing = pl.pallas_call(
        select_kernel,
        out_shape=jax.ShapeDtypeStruct((NEAR, SENT, TILE), bf16),
        in_specs=[VMEM],
        out_specs=ANY,
        scratch_shapes=[
            pltpu.VMEM((H * 8, TILE), jnp.int32),
            pltpu.SMEM((H * 8, TILE), jnp.int32),
            pltpu.VMEM((NEAR, SENT, TILE), bf16),
            pltpu.SemaphoreType.DMA,
            pltpu.SemaphoreType.DMA((NEAR,)),
        ],
        compiler_params=params,
        cost_estimate=pl.CostEstimate(flops=0, bytes_accessed=6_000_000, transcendentals=0),
        name="select",
    )(gathered)
    outgoing, feat = lax.optimization_barrier((outgoing, feat))
    received = lax.all_to_all(outgoing, ("y", "l", "c"), split_axis=0, concat_axis=0, tiled=True)
    base, early = pl.pallas_call(
        fetch_kernel,
        out_shape=(pltpu.VMEM((BLOCKS, TILE), f32), pltpu.VMEM((EARLY, TILE, TILE), bf16)),
        in_specs=[VMEM, VMEM, ANY],
        out_specs=(VMEM, ANY),
        scratch_shapes=[pltpu.SemaphoreType.DMA],
        compiler_params=params,
        cost_estimate=pl.CostEstimate(flops=8_400_000, bytes_accessed=3_000_000, transcendentals=0),
        name="fetch",
    )(in_hbm(feat), in_hbm(local_tiles), in_hbm(stripe_tiles))
    aggregated = pl.pallas_call(
        stripe_kernel,
        out_shape=jax.ShapeDtypeStruct((COL * W, ROWB * TILE), bf16),
        in_specs=[SMEM, SMEM, SMEM, SMEM, VMEM, VMEM, VMEM, ANY, ANY],
        out_specs=VMEM,
        scratch_shapes=[
            pltpu.VMEM((ROWB, 2, TILE, TILE), bf16),
            pltpu.VMEM((CAP - EARLY, TILE, TILE), bf16),
            pltpu.VMEM((ROWB + 1, TILE, W), f32),
            pltpu.SemaphoreType.DMA,
            pltpu.SemaphoreType.DMA((PARTS,)),
        ],
        compiler_params=params,
        name="stripes",
    )(
        hub_ref,
        stripe_slot,
        stripe_target,
        stripe_live,
        received.reshape(NEAR * SENT, TILE),
        in_vmem(base),
        in_vmem(early),
        in_hbm(hub_tiles),
        in_hbm(stripe_tiles),
    )
    full = lax.all_to_all(aggregated, "x", split_axis=0, concat_axis=0, tiled=True)
    weight_cols = lax.dynamic_slice_in_dim(weight, lax.axis_index("x") * W, W, 1)
    result = jnp.dot(weight_cols.T, full, preferred_element_type=f32)
    return result.astype(bf16).T


def solution(mesh):
    split = Mesh(mesh.devices.reshape(Y, H, L, C, COL), ("y", "h", "l", "c", "x"))
    node = ("y", "h", "l", "c")
    in_specs = (
        P(node, "x"),
        P(node, None, None),
        P(node, None, None, None),
        P(node, None),
        P(node),
        P(node, None),
        P(node, None, None),
        P(node, None),
        P(node, None),
        P(node),
        P(),
    )
    return jax.shard_map(local, mesh=split, in_specs=in_specs, out_specs=P(node, "x"), check_vma=False)
```

time: 98.4 us -> 92.2 us (0.937)
  waiting for transfers between devices: 7.82 us -> 28.9 us
  blocking collectives: 52.2 us -> 34.3 us
  starting transfers between devices: 20.2 us -> 14.2 us
  local copies, waits for them, and re-layouts: 7.28 us -> 2.35 us
  Pallas kernels: 8.02 us -> 9.75 us
    all_gather x2 -> x0, blocking collectives: 26.9 us -> none  [the longest x1 16.4 us: local(): hubs_own = lax.all_gather(hubs_l, 'y', axis=0, tiled=True)]
    all_to_all x1, waiting for transfers between devices: 1.86 us -> 23.4 us  [local(): lax.all_to_all(outgoing, ('y', 'l', 'c'), split_axis=0, concat_axis=0, ti...]
    all_gather x1, blocking collectives: 25.3 us -> 34.3 us  [local(): gathered = lax.all_gather(payload, 'h', axis=0, tiled=True)]
    unnamed x19 -> x15, local copies, waits for them, and re-layouts: 7.28 us -> 2.35 us
    ppermute x1 -> x0, starting transfers between devices: 4.13 us -> none  [local(): hubs_other = lax.ppermute(hubs_own, 'c', [(0, 1), (1, 0)])]
    all_to_all x1, starting transfers between devices: 12 us -> 10.2 us  [local(): lax.all_to_all(outgoing, ('y', 'l', 'c'), split_axis=0, concat_axis=0, ti...]
    pallas_call x2, Pallas kernels: 3.2 us -> 4.95 us  [the longest x1 2.62 us: local(): pl.pallas_call(select_kernel, out_shape=jax.ShapeDtypeStruct((NEAR, SENT,...]
  transfers between devices with their start and end apart: 3 -> 2, of which waited for: 3 -> 2; matrix products, arithmetic and copies ran while one was open for 1% -> 0% of each run, Pallas kernels for 1% -> 3%
where the time goes in v2:
time: 92.2 us; the launch traced here: 91.7 us
  blocking collectives  34.3 us (37%)
  waiting for transfers between devices  28.9 us (31%)
  starting transfers between devices  14.2 us (15%)
  Pallas kernels  9.75 us (11%)
  local copies, waits for them, and re-layouts  2.35 us (3%)
  between operations  1.39 us (2%)
    all_gather x1, blocking collectives, local(): gathered = lax.all_gather(payload, 'h', axis=0, tiled=True)  34.3 us
    all_to_all x1, waiting for transfers between devices, local(): lax.all_to_all(outgoing, ('y', 'l', 'c'), split_axis=0, concat_axis=0, ti...  23.4 us
    all_to_all x1, starting transfers between devices, local(): lax.all_to_all(outgoing, ('y', 'l', 'c'), split_axis=0, concat_axis=0, ti...  10.2 us
    all_to_all x1, waiting for transfers between devices, local(): lax.all_to_all(aggregated, 'x', split_axis=0, concat_axis=0, tiled=True)  5.53 us
    all_to_all x1, starting transfers between devices, local(): lax.all_to_all(aggregated, 'x', split_axis=0, concat_axis=0, tiled=True)  4.02 us
    pallas_call x1, Pallas kernels, local(): pl.pallas_call(stripe_kernel, out_shape=jax.ShapeDtypeStruct((COL * W, RO...  3.95 us
    pallas_call x1, Pallas kernels, local(): pl.pallas_call(select_kernel, out_shape=jax.ShapeDtypeStruct((NEAR, SENT,...  2.62 us
    unnamed x15, local copies, waits for them, and re-layouts  2.35 us
  transfers between devices with their start and end apart: 2, of which 2 were waited for; matrix products, arithmetic and copies ran while one was open for 0% of the time, Pallas kernels for 3%

profile of v2, /device:TPU:1, one launch (start us, length us, event | category | flops | bytes accessed | tf_op | source)
XLA Modules:
  0.0 91.7 jit_solution(12633502616630889637)
XLA Ops:
  0.0 0.0 copy-start
  0.7 0.9 pack.1
  1.5 34.3 %all_gather.3.gathered = bf16[2432,128]{1,0:T(8,128)(2,1)S(1)} all-gather(bf16[304,128]{1,0:T(8,128)(2,1)S(1)} %pack.1), channel_id=1, replica_groups=mesh['y'=4,'h'=8,'l'=2,'c'=2,'x'=4] {'h'}, dimensions={0}, use_global_device_ids=true | all-gather | bytes 700416 | tf_op jit(solution)/shard_map/all_gather | solution.py:145
  35.8 2.6 %select.1 = bf16[16,512,128]{2,1,0:T(8,128)(2,1)} custom-call(bf16[2432,128]{1,0:T(8,128)(2,1)S(1)} %all_gather.3.gathered), custom_call_target="tpu_custom_call" | custom-call | bytes 6000000 | tf_op jit(solution)/shard_map/select/pallas_call | solution.py:146
  38.4 0.0 copy-start.6
  38.4 10.2 %all-to-all-start = ((bf16[16,512,128]{2,1,0:T(8,128)(2,1)}), bf16[16,512,128]{2,1,0:T(8,128)(2,1)S(1)}, u32[]{:S(2)}, u32[]{:S(2)}) async-start(bf16[16,512,128]{2,1,0:T(8,128)(2,1)} %select.1), calls=%async_computation | async-start | bytes 4194304 | tf_op jit(solution)/shard_map/all_to_all | solution.py:163
  48.6 0.0 copy-done.6
  48.6 0.1 copy.12.hub_ref
  49.3 0.0 copy-start.4
  49.3 0.0 copy-start.5
  49.3 2.3 %fetch.1 = (f32[256,128]{1,0:T(8,128)S(1)}, bf16[40,128,128]{2,1,0:T(8,128)(2,1)S(1)}) custom-call(bf16[32,1024]{1,0:T(8,128)(2,1)} %bitcast.9, bf16[8,128,128]{2,1,0:T(8,128)(2,1)} %local_tiles.1, bf16[128,128,128]{2,1,0:T(8,128)(2,1)} %tiles_hbm.3), custom_call_target="tpu_custom_call" | custom-call | flops 8400000 | bytes 3000000 | tf_op jit(solution)/shard_map/fetch/pallas_call | solution.py:164
  51.7 0.0 copy-start.2
  51.7 0.6 copy-done.2
  52.3 23.4 %all-to-all-done = bf16[16,512,128]{2,1,0:T(8,128)(2,1)S(1)} async-done(((bf16[16,512,128]{2,1,0:T(8,128)(2,1)}), bf16[16,512,128]{2,1,0:T(8,128)(2,1)S(1)}, u32[]{:S(2)}, u32[]{:S(2)}) %all-to-all-start) | async-done | bytes 2097184 | tf_op jit(solution)/shard_map/all_to_all | solution.py:163
  75.7 0.0 copy-done.4
  75.7 0.0 copy-done.5
  75.7 0.0 copy-start.3
  75.7 0.9 copy-done.3
  76.6 3.9 %stripes.1 = bf16[128,1024]{1,0:T(8,128)(2,1)S(1)} custom-call(s32[8,2]{1,0:T(8,128)S(1)} %copy.12.hub_ref, s32[1,128]{1,0:T(1,128)S(1)} %copy-done.4, s32[1,128]{1,0:T(1,128)S(1)} %copy-done.5, s32[1]{0:T(128)S(6)} %copy.14.live, bf16[8192,128]{1,0:T(8,128)(2,1)S(1)} %bitcast.5, f32[256,128]{1,0:T(8,128)S(1)} %copy-done.3, ...), custom_call_target="tpu_custom_call" | custom-call | tf_op jit(solution)/shard_map/stripes/pallas_call | solution.py:174
  80.6 0.0 copy-start.1
  80.6 0.7 copy-done.1
  81.3 4.0 %all-to-all-start.1 = ((bf16[4,32,1024]{2,1,0:T(8,128)(2,1)}), bf16[4,32,1024]{2,1,0:T(8,128)(2,1)S(1)}, u32[]{:S(2)}, u32[]{:S(2)}) async-start(bf16[4,32,1024]{2,1,0:T(8,128)(2,1)} %bitcast.6), calls=%async_computation.1 | async-start | bytes 524288 | tf_op jit(solution)/shard_map/all_to_all | solution.py:199
  85.3 5.5 %all-to-all-done.1 = bf16[4,32,1024]{2,1,0:T(8,128)(2,1)S(1)} async-done(((bf16[4,32,1024]{2,1,0:T(8,128)(2,1)}), bf16[4,32,1024]{2,1,0:T(8,128)(2,1)S(1)}, u32[]{:S(2)}, u32[]{:S(2)}) %all-to-all-start.1) | async-done | bytes 262176 | tf_op jit(solution)/shard_map/all_to_all | solution.py:199
  90.8 0.0 copy-done
  90.8 0.9 convolution_convert_fusion
Async XLA Ops:
  0.0 90.8 %copy-start = (bf16[128,128]{1,0:T(8,128)(2,1)S(1)}, bf16[128,128]{1,0:T(8,128)(2,1)}, u32[]{:S(2)}) copy-start(bf16[128,128]{1,0:T(8,128)(2,1)} %param.21) | copy-start | bytes 98308
  38.4 10.2 %copy-start.6 = (s32[8,2]{0,1:T(2,128)S(1)}, s32[8,2]{0,1:T(2,128)}, u32[]{:S(2)}) copy-start(s32[8,2]{0,1:T(2,128)} %param.14) | copy-start | bytes 196
  38.4 37.3 %all-to-all-start = ((bf16[16,512,128]{2,1,0:T(8,128)(2,1)}), bf16[16,512,128]{2,1,0:T(8,128)(2,1)S(1)}, u32[]{:S(2)}, u32[]{:S(2)}) async-start(bf16[16,512,128]{2,1,0:T(8,128)(2,1)} %select.1), calls=%async_computation | async-start | bytes 4194304 | tf_op jit(solution)/shard_map/all_to_all | solution.py:163
  49.3 26.4 %copy-start.4 = (s32[1,128]{1,0:T(1,128)S(1)}, s32[1,128]{1,0:T(1,128)}, u32[]{:S(2)}) copy-start(s32[1,128]{1,0:T(1,128)} %slot.1) | copy-start | bytes 1540
  49.3 26.4 %copy-start.5 = (s32[1,128]{1,0:T(1,128)S(1)}, s32[1,128]{1,0:T(1,128)}, u32[]{:S(2)}) copy-start(s32[1,128]{1,0:T(1,128)} %target.1) | copy-start | bytes 1540
  51.7 0.7 copy-start.2
  75.7 0.9 copy-start.3
  80.6 0.7 copy-start.1
  81.3 9.6 %all-to-all-start.1 = ((bf16[4,32,1024]{2,1,0:T(8,128)(2,1)}), bf16[4,32,1024]{2,1,0:T(8,128)(2,1)S(1)}, u32[]{:S(2)}, u32[]{:S(2)}) async-start(bf16[4,32,1024]{2,1,0:T(8,128)(2,1)} %bitcast.6), calls=%async_computation.1 | async-start | bytes 524288 | tf_op jit(solution)/shard_map/all_to_all | solution.py:199

commit v3 on v2

--- a/solution.py
+++ b/solution.py
@@ -44,7 +44,7 @@
 def select_kernel(gathered, out, index_vmem, index, buffer, sem, sems):
     for h in range(H):
         meta = gathered[h * PAY + META : (h + 1) * PAY, :].astype(jnp.float32)
-        index_vmem[h * 8 : h * 8 + 8, :] = meta[:8].astype(jnp.int32)
+        index_vmem[h : h + 1, :] = meta[:1].astype(jnp.int32)
     copy = pltpu.make_async_copy(index_vmem, index, sem)
     copy.start()
     for m in range(NEAR):
@@ -57,7 +57,7 @@
     for m in range(NEAR):
         reader = (m // (L * C)) * (H * L * C) + pair * (L * C) + m % (L * C)
         for h in range(H):
-            block = index[h * 8, reader]
+            block = index[h, reader]
             buffer[m, h * W : (h + 1) * W, :] = gathered[rows_of(h * PAY + block * W), :]
         copies.append(pltpu.make_async_copy(buffer.at[m], out.at[m], sems.at[m]))
         copies[-1].start()
@@ -145,12 +145,12 @@
     gathered = lax.all_gather(payload, "h", axis=0, tiled=True)
     outgoing = pl.pallas_call(
         select_kernel,
-        out_shape=jax.ShapeDtypeStruct((NEAR, SENT, TILE), bf16),
+        out_shape=pltpu.HBM((NEAR, SENT, TILE), bf16),
         in_specs=[VMEM],
         out_specs=ANY,
         scratch_shapes=[
-            pltpu.VMEM((H * 8, TILE), jnp.int32),
-            pltpu.SMEM((H * 8, TILE), jnp.int32),
+            pltpu.VMEM((H, TILE), jnp.int32),
+            pltpu.SMEM((H, TILE), jnp.int32),
             pltpu.VMEM((NEAR, SENT, TILE), bf16),
             pltpu.SemaphoreType.DMA,
             pltpu.SemaphoreType.DMA((NEAR,)),
@@ -163,7 +163,7 @@
     received = lax.all_to_all(outgoing, ("y", "l", "c"), split_axis=0, concat_axis=0, tiled=True)
     base, early = pl.pallas_call(
         fetch_kernel,
-        out_shape=(pltpu.VMEM((BLOCKS, TILE), f32), pltpu.VMEM((EARLY, TILE, TILE), bf16)),
+        out_shape=(pltpu.HBM((BLOCKS, TILE), f32), pltpu.VMEM((EARLY, TILE, TILE), bf16)),
         in_specs=[VMEM, VMEM, ANY],
         out_specs=(VMEM, ANY),
         scratch_shapes=[pltpu.SemaphoreType.DMA],
@@ -173,7 +173,7 @@
     )(in_hbm(feat), in_hbm(local_tiles), in_hbm(stripe_tiles))
     aggregated = pl.pallas_call(
         stripe_kernel,
-        out_shape=jax.ShapeDtypeStruct((COL * W, ROWB * TILE), bf16),
+        out_shape=pltpu.HBM((COL * W, ROWB * TILE), bf16),
         in_specs=[SMEM, SMEM, SMEM, SMEM, VMEM, VMEM, VMEM, ANY, ANY],
         out_specs=VMEM,
         scratch_shapes=[
@@ -191,7 +191,7 @@
         stripe_target,
         stripe_live,
         received.reshape(NEAR * SENT, TILE),
-        in_vmem(base),
+        in_hbm(base),
         in_vmem(early),
         in_hbm(hub_tiles),
         in_hbm(stripe_tiles),

time: 92.2 us -> 91.1 us (0.988)
  local copies, waits for them, and re-layouts: 2.35 us -> 0.1 us
  Pallas kernels: 9.75 us -> 11 us
    unnamed x15 -> x9, local copies, waits for them, and re-layouts: 2.35 us -> 0.1 us
    pallas_call x3, Pallas kernels: 8.89 us -> 10.1 us  [the longest x1 4.98 us: local(): pl.pallas_call(stripe_kernel, out_shape=pltpu.HBM((COL * W, ROWB * TILE),...]
where the time goes in v3:
time: 91.1 us; the launch traced here: 90.7 us
  blocking collectives  34.3 us (38%)
  waiting for transfers between devices  28.9 us (32%)
  starting transfers between devices  14.2 us (16%)
  Pallas kernels  11 us (12%)
  between operations  1.37 us (2%)
    all_gather x1, blocking collectives, local(): gathered = lax.all_gather(payload, 'h', axis=0, tiled=True)  34.3 us
    all_to_all x1, waiting for transfers between devices, local(): lax.all_to_all(outgoing, ('y', 'l', 'c'), split_axis=0, concat_axis=0, ti...  23.4 us
    all_to_all x1, starting transfers between devices, local(): lax.all_to_all(outgoing, ('y', 'l', 'c'), split_axis=0, concat_axis=0, ti...  10.2 us
    all_to_all x1, waiting for transfers between devices, local(): lax.all_to_all(aggregated, 'x', split_axis=0, concat_axis=0, tiled=True)  5.53 us
    pallas_call x1, Pallas kernels, local(): pl.pallas_call(stripe_kernel, out_shape=pltpu.HBM((COL * W, ROWB * TILE),...  4.98 us
    all_to_all x1, starting transfers between devices, local(): lax.all_to_all(aggregated, 'x', split_axis=0, concat_axis=0, tiled=True)  4.03 us
    pallas_call x1, Pallas kernels, local(): pl.pallas_call(fetch_kernel, out_shape=(pltpu.HBM((BLOCKS, TILE), f32), p...  2.97 us
    pallas_call x1, Pallas kernels, local(): pl.pallas_call(select_kernel, out_shape=pltpu.HBM((NEAR, SENT, TILE), bf1...  2.17 us
  transfers between devices with their start and end apart: 2, of which 2 were waited for; matrix products, arithmetic and copies ran while one was open for 0% of the time, Pallas kernels for 3%

profile of v3, /device:TPU:1, one launch (start us, length us, event | category | flops | bytes accessed | tf_op | source)
XLA Modules:
  0.0 90.7 jit_solution(2915949884969062977)
XLA Ops:
  0.0 0.0 copy-start
  0.7 0.9 pack.1
  1.5 34.3 %all_gather.3.gathered = bf16[2432,128]{1,0:T(8,128)(2,1)S(1)} all-gather(bf16[304,128]{1,0:T(8,128)(2,1)S(1)} %pack.1), channel_id=1, replica_groups=mesh['y'=4,'h'=8,'l'=2,'c'=2,'x'=4] {'h'}, dimensions={0}, use_global_device_ids=true | all-gather | bytes 700416 | tf_op jit(solution)/shard_map/all_gather | solution.py:145
  35.8 2.2 %select.1 = bf16[16,512,128]{2,1,0:T(8,128)(2,1)} custom-call(bf16[2432,128]{1,0:T(8,128)(2,1)S(1)} %all_gather.3.gathered), custom_call_target="tpu_custom_call" | custom-call | bytes 6000000 | tf_op jit(solution)/shard_map/select/pallas_call | solution.py:146
  38.0 0.0 copy-start.3
  38.0 10.2 %all-to-all-start = ((bf16[16,512,128]{2,1,0:T(8,128)(2,1)}), bf16[16,512,128]{2,1,0:T(8,128)(2,1)S(1)}, u32[]{:S(2)}, u32[]{:S(2)}) async-start(bf16[16,512,128]{2,1,0:T(8,128)(2,1)} %select.1), calls=%async_computation | async-start | bytes 4194304 | tf_op jit(solution)/shard_map/all_to_all | solution.py:163
  48.1 0.0 copy-done.3
  48.1 0.1 copy.12.hub_ref
  48.9 0.0 copy-start.1
  48.9 0.0 copy-start.2
  48.9 3.0 %fetch.1 = (f32[256,128]{1,0:T(8,128)}, bf16[40,128,128]{2,1,0:T(8,128)(2,1)S(1)}) custom-call(bf16[32,1024]{1,0:T(8,128)(2,1)} %bitcast.9, bf16[8,128,128]{2,1,0:T(8,128)(2,1)} %local_tiles.1, bf16[128,128,128]{2,1,0:T(8,128)(2,1)} %tiles_hbm.3), custom_call_target="tpu_custom_call" | custom-call | flops 8400000 | bytes 3000000 | tf_op jit(solution)/shard_map/fetch/pallas_call | solution.py:164
  51.9 23.4 %all-to-all-done = bf16[16,512,128]{2,1,0:T(8,128)(2,1)S(1)} async-done(((bf16[16,512,128]{2,1,0:T(8,128)(2,1)}), bf16[16,512,128]{2,1,0:T(8,128)(2,1)S(1)}, u32[]{:S(2)}, u32[]{:S(2)}) %all-to-all-start) | async-done | bytes 2097184 | tf_op jit(solution)/shard_map/all_to_all | solution.py:163
  75.2 0.0 copy-done.1
  75.2 0.0 copy-done.2
  75.2 5.0 %stripes.1 = bf16[128,1024]{1,0:T(8,128)(2,1)} custom-call(s32[8,2]{1,0:T(8,128)S(1)} %copy.12.hub_ref, s32[1,128]{1,0:T(1,128)S(1)} %copy-done.1, s32[1,128]{1,0:T(1,128)S(1)} %copy-done.2, s32[1]{0:T(128)S(6)} %copy.14.live, bf16[8192,128]{1,0:T(8,128)(2,1)S(1)} %bitcast.5, f32[256,128]{1,0:T(8,128)} %get-tuple-element.11.base, ...), custom_call_target="tpu_custom_call" | custom-call | tf_op jit(solution)/shard_map/stripes/pallas_call | solution.py:174
  80.2 4.0 %all-to-all-start.1 = ((bf16[4,32,1024]{2,1,0:T(8,128)(2,1)}), bf16[4,32,1024]{2,1,0:T(8,128)(2,1)S(1)}, u32[]{:S(2)}, u32[]{:S(2)}) async-start(bf16[4,32,1024]{2,1,0:T(8,128)(2,1)} %bitcast.6), calls=%async_computation.1 | async-start | bytes 524288 | tf_op jit(solution)/shard_map/all_to_all | solution.py:199
  84.3 5.5 %all-to-all-done.1 = bf16[4,32,1024]{2,1,0:T(8,128)(2,1)S(1)} async-done(((bf16[4,32,1024]{2,1,0:T(8,128)(2,1)}), bf16[4,32,1024]{2,1,0:T(8,128)(2,1)S(1)}, u32[]{:S(2)}, u32[]{:S(2)}) %all-to-all-start.1) | async-done | bytes 262176 | tf_op jit(solution)/shard_map/all_to_all | solution.py:199
  89.8 0.0 copy-done
  89.8 0.9 %convolution_convert_fusion = bf16[1024,32]{0,1:T(8,128)(2,1)} fusion(bf16[128,1024]{1,0:T(8,128)(2,1)S(1)} %bitcast.7, bf16[128,128]{1,0:T(8,128)(2,1)S(1)} %copy-done, s32[]{:T(128)S(6)} %select_n.3), kind=kOutput, calls=%fused_computation | convolution fusion | flops 8421376 | bytes 360452 | tf_op jit(solution)/shard_map/dot_general | solution.py:201
Async XLA Ops:
  0.0 89.8 %copy-start = (bf16[128,128]{1,0:T(8,128)(2,1)S(1)}, bf16[128,128]{1,0:T(8,128)(2,1)}, u32[]{:S(2)}) copy-start(bf16[128,128]{1,0:T(8,128)(2,1)} %param.21) | copy-start | bytes 98308
  38.0 10.2 %copy-start.3 = (s32[8,2]{0,1:T(2,128)S(1)}, s32[8,2]{0,1:T(2,128)}, u32[]{:S(2)}) copy-start(s32[8,2]{0,1:T(2,128)} %param.14) | copy-start | bytes 196
  38.0 37.3 %all-to-all-start = ((bf16[16,512,128]{2,1,0:T(8,128)(2,1)}), bf16[16,512,128]{2,1,0:T(8,128)(2,1)S(1)}, u32[]{:S(2)}, u32[]{:S(2)}) async-start(bf16[16,512,128]{2,1,0:T(8,128)(2,1)} %select.1), calls=%async_computation | async-start | bytes 4194304 | tf_op jit(solution)/shard_map/all_to_all | solution.py:163
  48.9 26.4 %copy-start.1 = (s32[1,128]{1,0:T(1,128)S(1)}, s32[1,128]{1,0:T(1,128)}, u32[]{:S(2)}) copy-start(s32[1,128]{1,0:T(1,128)} %slot.1) | copy-start | bytes 1540
  48.9 26.4 %copy-start.2 = (s32[1,128]{1,0:T(1,128)S(1)}, s32[1,128]{1,0:T(1,128)}, u32[]{:S(2)}) copy-start(s32[1,128]{1,0:T(1,128)} %target.1) | copy-start | bytes 1540
  80.2 9.6 %all-to-all-start.1 = ((bf16[4,32,1024]{2,1,0:T(8,128)(2,1)}), bf16[4,32,1024]{2,1,0:T(8,128)(2,1)S(1)}, u32[]{:S(2)}, u32[]{:S(2)}) async-start(bf16[4,32,1024]{2,1,0:T(8,128)(2,1)} %bitcast.6), calls=%async_computation.1 | async-start | bytes 524288 | tf_op jit(solution)/shard_map/all_to_all | solution.py:199

commit v4 on v3

v4 whole, which is shorter than its diff:
```python
import jax
import jax.numpy as jnp
from jax import lax
from jax.experimental import pallas as pl
from jax.experimental.pallas import tpu as pltpu
from jax.sharding import Mesh, PartitionSpec as P

Y, H, L, C, COL = 4, 8, 2, 2, 4
ROWB, TILE, W = 8, 128, 32
NEAR = Y * L
CAP = 128
EARLY = 96
BLOCKS = ROWB * W
PAY = BLOCKS + 16
SENT = (C + 1) * H * W
KEPT = 2 * H * W
NT = (((1,), (1,)), ((), ()))
VMEM = pl.BlockSpec(memory_space=pltpu.VMEM)
SMEM = pl.BlockSpec(memory_space=pltpu.SMEM)
ANY = pl.BlockSpec(memory_space=pl.ANY)


def rows_of(start):
    return pl.ds(pl.multiple_of(start, 16), W)


def in_hbm(array):
    return pltpu.with_memory_space_constraint(array, pltpu.HBM)


def in_vmem(array):
    return pltpu.with_memory_space_constraint(array, pltpu.VMEM)


def pack_kernel(hub_list, feat, send, out):
    for b in range(ROWB):
        out[b * W : (b + 1) * W, :] = feat[:, b * TILE : (b + 1) * TILE]
    row = lax.broadcasted_iota(jnp.int32, (16, TILE), 0)
    meta = jnp.where(row == 0, jnp.broadcast_to(send[...], (16, TILE)), hub_list[0])
    out[BLOCKS:PAY, :] = meta.astype(jnp.float32).astype(jnp.bfloat16)


def select_kernel(gathered, out, index_vmem, index, buffer, sem, sems):
    for h in range(H):
        meta = gathered[h * PAY + BLOCKS : (h + 1) * PAY, :].astype(jnp.float32)
        index_vmem[2 * h : 2 * h + 2, :] = meta[:2].astype(jnp.int32)
    copy = pltpu.make_async_copy(index_vmem, index, sem)
    copy.start()
    copy.wait()
    pair = lax.axis_index("h")
    hubs = [gathered[rows_of(h * PAY + index[2 * h + 1, 0] * W), :] for h in range(H)]
    copies = []
    for m in range(NEAR):
        for c in range(C):
            reader = (m // L) * (H * L * C) + pair * (L * C) + (m % L) * C + c
            for h in range(H):
                block = index[2 * h, reader]
                at = (c * H + h) * W
                buffer[m, at : at + W, :] = gathered[rows_of(h * PAY + block * W), :]
        for h in range(H):
            at = (C * H + h) * W
            buffer[m, at : at + W, :] = hubs[h]
        copies.append(pltpu.make_async_copy(buffer.at[m], out.at[m], sems.at[m]))
        copies[-1].start()
    for copy in copies:
        copy.wait()


def fetch_kernel(feat, local_tiles, tiles_hbm, out, tiles, sem):
    copy = pltpu.make_async_copy(tiles_hbm.at[pl.ds(0, EARLY)], tiles, sem)
    copy.start()
    for b in range(ROWB):
        out[b * W : (b + 1) * W, :] = lax.dot_general(
            feat[:, b * TILE : (b + 1) * TILE], local_tiles[b], NT, preferred_element_type=jnp.float32
        )
    copy.wait()


def stripe_kernel(
    hub_ref, slot, target, live, own, other, base, early, hub_hbm, tiles_hbm, out, blocks, hub_tiles, late, acc, sems
):
    core = lax.axis_index("c")
    half = H * W
    copies = []
    for k, (source, place) in enumerate(((own, core), (other, 1 - core))):
        for part in range(2):
            rows = pl.ds(core * half, half) if part == 0 else pl.ds(C * half, half)
            into = blocks.at[pl.ds(place * NEAR, NEAR), pl.ds(part * half, half)]
            copies.append(pltpu.make_async_copy(source.at[:, rows], into, sems.at[2 * k + part]))
    copies.append(pltpu.make_async_copy(tiles_hbm.at[pl.ds(EARLY, CAP - EARLY)], late, sems.at[4]))
    copies.append(pltpu.make_async_copy(hub_hbm, hub_tiles, sems.at[5]))
    for k in (0, 2, 1, 3, 4, 5):
        copies[k].start()

    def product(tile, node, first):
        near = (node & 1) * NEAR + lax.shift_right_logical(node, 5) * L + (lax.shift_right_logical(node, 1) & 1)
        rows = rows_of(first + (lax.shift_right_logical(node, 2) & 7) * W)
        return lax.dot_general(tile, blocks[near, rows, :], NT, preferred_element_type=jnp.float32)

    for b in range(ROWB + 1):
        acc[b] = jnp.zeros((TILE, W), jnp.float32)
    count = live[0]
    copies[0].wait()
    copies[2].wait()
    for s in range(CAP):
        if s == EARLY:
            copies[4].wait()
        tile = early[s] if s < EARLY else late[s - EARLY]
        row = jnp.where(s < count, target[0, s], ROWB)
        acc[row] += product(tile, slot[0, s], 0)
    for k in (1, 3, 5):
        copies[k].wait()
    for b in range(ROWB):
        total = acc[b]
        for j in range(2):
            total += product(hub_tiles[b, j], hub_ref[b, j], half)
        agg = (total.T + base[b * W : (b + 1) * W, :]).astype(jnp.bfloat16)
        for k in range(COL):
            out[k * W : (k + 1) * W, b * TILE : (b + 1) * TILE] = agg


def local(
    features,
    local_tiles,
    hub_tiles,
    hub_ref,
    hub_list,
    send_list,
    stripe_tiles,
    stripe_slot,
    stripe_target,
    stripe_live,
    weight,
):
    bf16, f32 = jnp.bfloat16, jnp.float32
    params = pltpu.CompilerParams(vmem_limit_bytes=16 * 1024 * 1024)
    feat = features.T
    payload = pl.pallas_call(
        pack_kernel,
        out_shape=jax.ShapeDtypeStruct((PAY, TILE), bf16),
        in_specs=[SMEM, VMEM, VMEM],
        out_specs=VMEM,
        compiler_params=params,
        name="pack",
    )(hub_list, in_hbm(feat), in_hbm(send_list))
    gathered = lax.all_gather(payload, "h", axis=0, tiled=True)
    outgoing = pl.pallas_call(
        select_kernel,
        out_shape=pltpu.HBM((NEAR, SENT, TILE), bf16),
        in_specs=[VMEM],
        out_specs=ANY,
        scratch_shapes=[
            pltpu.VMEM((2 * H, TILE), jnp.int32),
            pltpu.SMEM((2 * H, TILE), jnp.int32),
            pltpu.VMEM((NEAR, SENT, TILE), bf16),
            pltpu.SemaphoreType.DMA,
            pltpu.SemaphoreType.DMA((NEAR,)),
        ],
        compiler_params=params,
        cost_estimate=pl.CostEstimate(flops=0, bytes_accessed=6_000_000, transcendentals=0),
        name="select",
    )(gathered)
    outgoing, feat = lax.optimization_barrier((outgoing, feat))
    received = lax.all_to_all(outgoing, ("y", "l"), split_axis=0, concat_axis=0, tiled=True)
    base, early = pl.pallas_call(
        fetch_kernel,
        out_shape=(pltpu.HBM((BLOCKS, TILE), f32), pltpu.VMEM((EARLY, TILE, TILE), bf16)),
        in_specs=[VMEM, VMEM, ANY],
        out_specs=(VMEM, ANY),
        scratch_shapes=[pltpu.SemaphoreType.DMA],
        compiler_params=params,
        cost_estimate=pl.CostEstimate(flops=8_400_000, bytes_accessed=3_000_000, transcendentals=0),
        name="fetch",
    )(in_hbm(feat), in_hbm(local_tiles), in_hbm(stripe_tiles))
    received, early = lax.optimization_barrier((received, early))
    other = lax.ppermute(received, "c", [(0, 1), (1, 0)])
    aggregated = pl.pallas_call(
        stripe_kernel,
        out_shape=pltpu.HBM((COL * W, ROWB * TILE), bf16),
        in_specs=[SMEM, SMEM, SMEM, SMEM, ANY, ANY, VMEM, VMEM, ANY, ANY],
        out_specs=VMEM,
        scratch_shapes=[
            pltpu.VMEM((C * NEAR, KEPT, TILE), bf16),
            pltpu.VMEM((ROWB, 2, TILE, TILE), bf16),
            pltpu.VMEM((CAP - EARLY, TILE, TILE), bf16),
            pltpu.VMEM((ROWB + 1, TILE, W), f32),
            pltpu.SemaphoreType.DMA((6,)),
        ],
        compiler_params=params,
        name="stripes",
    )(
        hub_ref,
        stripe_slot,
        stripe_target,
        stripe_live,
        in_hbm(received),
        in_hbm(other),
        in_hbm(base),
        in_vmem(early),
        in_hbm(hub_tiles),
        in_hbm(stripe_tiles),
    )
    full = lax.all_to_all(aggregated, "x", split_axis=0, concat_axis=0, tiled=True)
    weight_cols = lax.dynamic_slice_in_dim(weight, lax.axis_index("x") * W, W, 1)
    result = jnp.dot(weight_cols.T, full, preferred_element_type=f32)
    return result.astype(bf16).T


def solution(mesh):
    split = Mesh(mesh.devices.reshape(Y, H, L, C, COL), ("y", "h", "l", "c", "x"))
    node = ("y", "h", "l", "c")
    in_specs = (
        P(node, "x"),
        P(node, None, None),
        P(node, None, None, None),
        P(node, None),
        P(node),
        P(node, None),
        P(node, None, None),
        P(node, None),
        P(node, None),
        P(node),
        P(),
    )
    return jax.shard_map(local, mesh=split, in_specs=in_specs, out_specs=P(node, "x"), check_vma=False)
```

time: 91.1 us -> 85 us (0.933)
  waiting for transfers between devices: 28.9 us -> 20.3 us
  starting transfers between devices: 14.2 us -> 17.6 us
  blocking collectives: 34.3 us -> 33.2 us
    all_to_all x1, waiting for transfers between devices: 23.4 us -> 11.9 us  [local(): lax.all_to_all(outgoing, ('y', 'l'), split_axis=0, concat_axis=0, tiled=T...]
    ppermute x0 -> x1, starting transfers between devices: none -> 8.92 us  [local(): other = lax.ppermute(received, 'c', [(0, 1), (1, 0)])]
    all_to_all x1, starting transfers between devices: 10.2 us -> 4.67 us  [local(): lax.all_to_all(outgoing, ('y', 'l'), split_axis=0, concat_axis=0, tiled=T...]
    ppermute x0 -> x1, waiting for transfers between devices: none -> 2.61 us  [local(): other = lax.ppermute(received, 'c', [(0, 1), (1, 0)])]
    all_gather x1, blocking collectives: 34.3 us -> 33.2 us  [local(): gathered = lax.all_gather(payload, 'h', axis=0, tiled=True)]
  transfers between devices with their start and end apart: 2 -> 3, of which waited for: 2 -> 3; matrix products, arithmetic and copies ran while one was open for 0% -> 0% of each run, Pallas kernels for 3% -> 4%
where the time goes in v4:
time: 85 us; the launch traced here: 84.6 us
  blocking collectives  33.2 us (39%)
  waiting for transfers between devices  20.3 us (24%)
  starting transfers between devices  17.6 us (21%)
  Pallas kernels  11 us (13%)
  between operations  1.38 us (2%)
  matrix products  0.91 us (1%)
    all_gather x1, blocking collectives, local(): gathered = lax.all_gather(payload, 'h', axis=0, tiled=True)  33.2 us
    all_to_all x1, waiting for transfers between devices, local(): lax.all_to_all(outgoing, ('y', 'l'), split_axis=0, concat_axis=0, tiled=T...  11.9 us
    ppermute x1, starting transfers between devices, local(): other = lax.ppermute(received, 'c', [(0, 1), (1, 0)])  8.92 us
    all_to_all x1, waiting for transfers between devices, local(): lax.all_to_all(aggregated, 'x', split_axis=0, concat_axis=0, tiled=True)  5.81 us
    pallas_call x1, Pallas kernels, local(): pl.pallas_call(stripe_kernel, out_shape=pltpu.HBM((COL * W, ROWB * TILE),...  4.69 us
    all_to_all x1, starting transfers between devices, local(): lax.all_to_all(outgoing, ('y', 'l'), split_axis=0, concat_axis=0, tiled=T...  4.67 us
    all_to_all x1, starting transfers between devices, local(): lax.all_to_all(aggregated, 'x', split_axis=0, concat_axis=0, tiled=True)  4.03 us
    pallas_call x1, Pallas kernels, local(): pl.pallas_call(fetch_kernel, out_shape=(pltpu.HBM((BLOCKS, TILE), f32), p...  3.54 us
  transfers between devices with their start and end apart: 3, of which 3 were waited for; matrix products, arithmetic and copies ran while one was open for 0% of the time, Pallas kernels for 4%

profile of v4, /device:TPU:1, one launch (start us, length us, event | category | flops | bytes accessed | tf_op | source)
XLA Modules:
  0.0 84.6 jit_solution(9347116643523766551)
XLA Ops:
  0.0 0.0 copy-start
  0.7 0.9 %pack.1 = bf16[272,128]{1,0:T(8,128)(2,1)S(1)} custom-call(s32[1]{0:T(128)S(6)} %copy.13.hub_list, bf16[32,1024]{1,0:T(8,128)(2,1)} %bitcast.6, s32[1,128]{1,0:T(1,128)} %send.1), custom_call_target="tpu_custom_call" | custom-call | tf_op jit(solution)/shard_map/pack/pallas_call | solution.py:138
  1.5 33.2 %all_gather.3.gathered = bf16[2176,128]{1,0:T(8,128)(2,1)S(1)} all-gather(bf16[272,128]{1,0:T(8,128)(2,1)S(1)} %pack.1), channel_id=1, replica_groups=mesh['y'=4,'h'=8,'l'=2,'c'=2,'x'=4] {'h'}, dimensions={0}, use_global_device_ids=true | all-gather | bytes 626688 | tf_op jit(solution)/shard_map/all_gather | solution.py:146
  34.7 2.0 %select.1 = bf16[8,768,128]{2,1,0:T(8,128)(2,1)} custom-call(bf16[2176,128]{1,0:T(8,128)(2,1)S(1)} %all_gather.3.gathered), custom_call_target="tpu_custom_call" | custom-call | bytes 6000000 | tf_op jit(solution)/shard_map/select/pallas_call | solution.py:147
  36.7 4.7 %all-to-all-start = ((bf16[8,768,128]{2,1,0:T(8,128)(2,1)}), bf16[8,768,128]{2,1,0:T(8,128)(2,1)}, u32[]{:S(2)}, u32[]{:S(2)}) async-start(bf16[8,768,128]{2,1,0:T(8,128)(2,1)} %select.1), calls=%async_computation | async-start | bytes 3145728 | tf_op jit(solution)/shard_map/all_to_all | solution.py:164
  41.4 0.0 copy-start.3
  41.4 0.0 copy-start.1
  41.4 0.0 copy-start.2
  41.4 3.5 %fetch.1 = (f32[256,128]{1,0:T(8,128)}, bf16[96,128,128]{2,1,0:T(8,128)(2,1)S(1)}) custom-call(bf16[32,1024]{1,0:T(8,128)(2,1)} %bitcast.7, bf16[8,128,128]{2,1,0:T(8,128)(2,1)} %local_tiles.1, bf16[128,128,128]{2,1,0:T(8,128)(2,1)} %tiles_hbm.3), custom_call_target="tpu_custom_call" | custom-call | flops 8400000 | bytes 3000000 | tf_op jit(solution)/shard_map/fetch/pallas_call | solution.py:165
  44.9 11.9 %all-to-all-done.own = bf16[8,768,128]{2,1,0:T(8,128)(2,1)} async-done(((bf16[8,768,128]{2,1,0:T(8,128)(2,1)}), bf16[8,768,128]{2,1,0:T(8,128)(2,1)}, u32[]{:S(2)}, u32[]{:S(2)}) %all-to-all-start) | async-done | bytes 1572896 | tf_op jit(solution)/shard_map/all_to_all | solution.py:164
  56.8 8.9 %collective-permute-start = (bf16[8,768,128]{2,1,0:T(8,128)(2,1)}, bf16[8,768,128]{2,1,0:T(8,128)(2,1)}, u32[]{:S(2)}, u32[]{:S(2)}) collective-permute-start(bf16[8,768,128]{2,1,0:T(8,128)(2,1)} %all-to-all-done.own), channel_id=1, source_target_pairs={{0,4},{4,0},{1,5},{5,1},{2,6},{6,2},{3,7},{7,3},{8,12},{12,8},{9,1... | collective-permute-start | bytes 4718600 | tf_op jit(solution)/shard_map/ppermute | solution.py:176
  65.7 0.0 copy-done.3
  65.7 0.1 copy.12.hub_ref
  66.5 2.6 %collective-permute-done.other = bf16[8,768,128]{2,1,0:T(8,128)(2,1)} collective-permute-done((bf16[8,768,128]{2,1,0:T(8,128)(2,1)}, bf16[8,768,128]{2,1,0:T(8,128)(2,1)}, u32[]{:S(2)}, u32[]{:S(2)}) %collective-permute-start) | collective-permute-done | bytes 1572896 | tf_op jit(solution)/shard_map/ppermute | solution.py:176
  69.1 0.0 copy-done.1
  69.1 0.0 copy-done.2
  69.1 4.7 %stripes.1 = bf16[128,1024]{1,0:T(8,128)(2,1)} custom-call(s32[8,2]{1,0:T(8,128)S(1)} %copy.12.hub_ref, s32[1,128]{1,0:T(1,128)S(1)} %copy-done.1, s32[1,128]{1,0:T(1,128)S(1)} %copy-done.2, s32[1]{0:T(128)S(6)} %copy.14.live, bf16[8,768,128]{2,1,0:T(8,128)(2,1)} %all-to-all-done.own, bf16[8,768,128]{2,1,0:T(8,128)(2,1)} %collective-permute-done.other, ...), custom_call_target="tpu_custom_call" | custom-call | tf_op jit(solution)/shard_map/stripes/pallas_call | solution.py:177
  73.8 4.0 %all-to-all-start.1 = ((bf16[4,32,1024]{2,1,0:T(8,128)(2,1)}), bf16[4,32,1024]{2,1,0:T(8,128)(2,1)S(1)}, u32[]{:S(2)}, u32[]{:S(2)}) async-start(bf16[4,32,1024]{2,1,0:T(8,128)(2,1)} %bitcast.4), calls=%async_computation.1 | async-start | bytes 524288 | tf_op jit(solution)/shard_map/all_to_all | solution.py:203
  77.8 5.8 %all-to-all-done.1 = bf16[4,32,1024]{2,1,0:T(8,128)(2,1)S(1)} async-done(((bf16[4,32,1024]{2,1,0:T(8,128)(2,1)}), bf16[4,32,1024]{2,1,0:T(8,128)(2,1)S(1)}, u32[]{:S(2)}, u32[]{:S(2)}) %all-to-all-start.1) | async-done | bytes 262176 | tf_op jit(solution)/shard_map/all_to_all | solution.py:203
  83.6 0.0 copy-done
  83.6 0.9 %convolution_convert_fusion = bf16[1024,32]{0,1:T(8,128)(2,1)} fusion(bf16[128,1024]{1,0:T(8,128)(2,1)S(1)} %bitcast.5, bf16[128,128]{1,0:T(8,128)(2,1)S(1)} %copy-done, s32[]{:T(128)S(6)} %select_n.3), kind=kOutput, calls=%fused_computation | convolution fusion | flops 8421376 | bytes 360452 | tf_op jit(solution)/shard_map/dot_general | solution.py:205
Async XLA Ops:
  0.0 83.6 %copy-start = (bf16[128,128]{1,0:T(8,128)(2,1)S(1)}, bf16[128,128]{1,0:T(8,128)(2,1)}, u32[]{:S(2)}) copy-start(bf16[128,128]{1,0:T(8,128)(2,1)} %param.21) | copy-start | bytes 98308
  36.7 20.1 %all-to-all-start = ((bf16[8,768,128]{2,1,0:T(8,128)(2,1)}), bf16[8,768,128]{2,1,0:T(8,128)(2,1)}, u32[]{:S(2)}, u32[]{:S(2)}) async-start(bf16[8,768,128]{2,1,0:T(8,128)(2,1)} %select.1), calls=%async_computation | async-start | bytes 3145728 | tf_op jit(solution)/shard_map/all_to_all | solution.py:164
  41.4 24.4 %copy-start.3 = (s32[8,2]{0,1:T(2,128)S(1)}, s32[8,2]{0,1:T(2,128)}, u32[]{:S(2)}) copy-start(s32[8,2]{0,1:T(2,128)} %param.14) | copy-start | bytes 196
  41.4 27.7 %copy-start.1 = (s32[1,128]{1,0:T(1,128)S(1)}, s32[1,128]{1,0:T(1,128)}, u32[]{:S(2)}) copy-start(s32[1,128]{1,0:T(1,128)} %slot.1) | copy-start | bytes 1540
  41.4 27.7 %copy-start.2 = (s32[1,128]{1,0:T(1,128)S(1)}, s32[1,128]{1,0:T(1,128)}, u32[]{:S(2)}) copy-start(s32[1,128]{1,0:T(1,128)} %target.1) | copy-start | bytes 1540
  56.8 12.3 %collective-permute-start = (bf16[8,768,128]{2,1,0:T(8,128)(2,1)}, bf16[8,768,128]{2,1,0:T(8,128)(2,1)}, u32[]{:S(2)}, u32[]{:S(2)}) collective-permute-start(bf16[8,768,128]{2,1,0:T(8,128)(2,1)} %all-to-all-done.own), channel_id=1, source_target_pairs={{0,4},{4,0},{1,5},{5,1},{2,6},{6,2},{3,7},{7,3},{8,12},{12,8},{9,1... | collective-permute-start | bytes 4718600 | tf_op jit(solution)/shard_map/ppermute | solution.py:176
  73.8 9.8 %all-to-all-start.1 = ((bf16[4,32,1024]{2,1,0:T(8,128)(2,1)}), bf16[4,32,1024]{2,1,0:T(8,128)(2,1)S(1)}, u32[]{:S(2)}, u32[]{:S(2)}) async-start(bf16[4,32,1024]{2,1,0:T(8,128)(2,1)} %bitcast.4), calls=%async_computation.1 | async-start | bytes 524288 | tf_op jit(solution)/shard_map/all_to_all | solution.py:203

commit v5 on v4

--- a/solution.py
+++ b/solution.py
@@ -52,7 +52,7 @@
     copies = []
     for m in range(NEAR):
         for c in range(C):
-            reader = (m // L) * (H * L * C) + pair * (L * C) + (m % L) * C + c
+            reader = (m % Y) * (H * L * C) + pair * (L * C) + (m // Y) * C + c
             for h in range(H):
                 block = index[2 * h, reader]
                 at = (c * H + h) * W
@@ -93,7 +93,7 @@
         copies[k].start()
 
     def product(tile, node, first):
-        near = (node & 1) * NEAR + lax.shift_right_logical(node, 5) * L + (lax.shift_right_logical(node, 1) & 1)
+        near = (node & 1) * NEAR + lax.shift_right_logical(node, 5) + (lax.shift_right_logical(node, 1) & 1) * Y
         rows = rows_of(first + (lax.shift_right_logical(node, 2) & 7) * W)
         return lax.dot_general(tile, blocks[near, rows, :], NT, preferred_element_type=jnp.float32)
 
@@ -161,7 +161,7 @@
         name="select",
     )(gathered)
     outgoing, feat = lax.optimization_barrier((outgoing, feat))
-    received = lax.all_to_all(outgoing, ("y", "l"), split_axis=0, concat_axis=0, tiled=True)
+    received = lax.all_to_all(outgoing, ("l", "y"), split_axis=0, concat_axis=0, tiled=True)
     base, early = pl.pallas_call(
         fetch_kernel,
         out_shape=(pltpu.HBM((BLOCKS, TILE), f32), pltpu.VMEM((EARLY, TILE, TILE), bf16)),

time: 85 us -> 84 us (0.988)
  starting transfers between devices: 17.6 us -> 16.7 us
    ppermute x1, starting transfers between devices: 8.92 us -> 7.97 us  [local(): other = lax.ppermute(received, 'c', [(0, 1), (1, 0)])]
where the time goes in v5:
time: 84 us; the launch traced here: 83.5 us
  blocking collectives  33.2 us (40%)
  waiting for transfers between devices  20.2 us (24%)
  starting transfers between devices  16.7 us (20%)
  Pallas kernels  11 us (13%)
  between operations  1.38 us (2%)
  matrix products  0.91 us (1%)
    all_gather x1, blocking collectives, local(): gathered = lax.all_gather(payload, 'h', axis=0, tiled=True)  33.2 us
    all_to_all x1, waiting for transfers between devices, local(): lax.all_to_all(outgoing, ('l', 'y'), split_axis=0, concat_axis=0, tiled=T...  11.8 us
    ppermute x1, starting transfers between devices, local(): other = lax.ppermute(received, 'c', [(0, 1), (1, 0)])  7.97 us
    all_to_all x1, waiting for transfers between devices, local(): lax.all_to_all(aggregated, 'x', split_axis=0, concat_axis=0, tiled=True)  5.79 us
    pallas_call x1, Pallas kernels, local(): pl.pallas_call(stripe_kernel, out_shape=pltpu.HBM((COL * W, ROWB * TILE),...  4.69 us
    all_to_all x1, starting transfers between devices, local(): lax.all_to_all(outgoing, ('l', 'y'), split_axis=0, concat_axis=0, tiled=T...  4.67 us
    all_to_all x1, starting transfers between devices, local(): lax.all_to_all(aggregated, 'x', split_axis=0, concat_axis=0, tiled=True)  4.02 us
    pallas_call x1, Pallas kernels, local(): pl.pallas_call(fetch_kernel, out_shape=(pltpu.HBM((BLOCKS, TILE), f32), p...  3.54 us
  transfers between devices with their start and end apart: 3, of which 3 were waited for; matrix products, arithmetic and copies ran while one was open for 0% of the time, Pallas kernels for 4%

profile of v5, /device:TPU:1, one launch (start us, length us, event | category | flops | bytes accessed | tf_op | source)
XLA Modules:
  0.0 83.5 jit_solution(4983226100114855449)
XLA Ops:
  0.0 0.0 copy-start
  0.7 0.9 %pack.1 = bf16[272,128]{1,0:T(8,128)(2,1)S(1)} custom-call(s32[1]{0:T(128)S(6)} %copy.13.hub_list, bf16[32,1024]{1,0:T(8,128)(2,1)} %bitcast.6, s32[1,128]{1,0:T(1,128)} %send.1), custom_call_target="tpu_custom_call" | custom-call | tf_op jit(solution)/shard_map/pack/pallas_call | solution.py:138
  1.5 33.2 %all_gather.3.gathered = bf16[2176,128]{1,0:T(8,128)(2,1)S(1)} all-gather(bf16[272,128]{1,0:T(8,128)(2,1)S(1)} %pack.1), channel_id=1, replica_groups=mesh['y'=4,'h'=8,'l'=2,'c'=2,'x'=4] {'h'}, dimensions={0}, use_global_device_ids=true | all-gather | bytes 626688 | tf_op jit(solution)/shard_map/all_gather | solution.py:146
  34.7 2.0 %select.1 = bf16[8,768,128]{2,1,0:T(8,128)(2,1)} custom-call(bf16[2176,128]{1,0:T(8,128)(2,1)S(1)} %all_gather.3.gathered), custom_call_target="tpu_custom_call" | custom-call | bytes 6000000 | tf_op jit(solution)/shard_map/select/pallas_call | solution.py:147
  36.7 4.7 %all-to-all-start = ((bf16[8,768,128]{2,1,0:T(8,128)(2,1)}), bf16[8,768,128]{2,1,0:T(8,128)(2,1)}, u32[]{:S(2)}, u32[]{:S(2)}) async-start(bf16[8,768,128]{2,1,0:T(8,128)(2,1)} %select.1), calls=%async_computation | async-start | bytes 3145728 | tf_op jit(solution)/shard_map/all_to_all | solution.py:164
  41.4 0.0 copy-start.3
  41.4 0.0 copy-start.1
  41.4 0.0 copy-start.2
  41.4 3.5 %fetch.1 = (f32[256,128]{1,0:T(8,128)}, bf16[96,128,128]{2,1,0:T(8,128)(2,1)S(1)}) custom-call(bf16[32,1024]{1,0:T(8,128)(2,1)} %bitcast.7, bf16[8,128,128]{2,1,0:T(8,128)(2,1)} %local_tiles.1, bf16[128,128,128]{2,1,0:T(8,128)(2,1)} %tiles_hbm.3), custom_call_target="tpu_custom_call" | custom-call | flops 8400000 | bytes 3000000 | tf_op jit(solution)/shard_map/fetch/pallas_call | solution.py:165
  44.9 11.8 %all-to-all-done.own = bf16[8,768,128]{2,1,0:T(8,128)(2,1)} async-done(((bf16[8,768,128]{2,1,0:T(8,128)(2,1)}), bf16[8,768,128]{2,1,0:T(8,128)(2,1)}, u32[]{:S(2)}, u32[]{:S(2)}) %all-to-all-start) | async-done | bytes 1572896 | tf_op jit(solution)/shard_map/all_to_all | solution.py:164
  56.8 8.0 %collective-permute-start = (bf16[8,768,128]{2,1,0:T(8,128)(2,1)}, bf16[8,768,128]{2,1,0:T(8,128)(2,1)}, u32[]{:S(2)}, u32[]{:S(2)}) collective-permute-start(bf16[8,768,128]{2,1,0:T(8,128)(2,1)} %all-to-all-done.own), channel_id=1, source_target_pairs={{0,4},{4,0},{1,5},{5,1},{2,6},{6,2},{3,7},{7,3},{8,12},{12,8},{9,1... | collective-permute-start | bytes 4718600 | tf_op jit(solution)/shard_map/ppermute | solution.py:176
  64.7 0.0 copy-done.3
  64.8 0.1 copy.12.hub_ref
  65.5 2.6 %collective-permute-done.other = bf16[8,768,128]{2,1,0:T(8,128)(2,1)} collective-permute-done((bf16[8,768,128]{2,1,0:T(8,128)(2,1)}, bf16[8,768,128]{2,1,0:T(8,128)(2,1)}, u32[]{:S(2)}, u32[]{:S(2)}) %collective-permute-start) | collective-permute-done | bytes 1572896 | tf_op jit(solution)/shard_map/ppermute | solution.py:176
  68.1 0.0 copy-done.1
  68.1 0.0 copy-done.2
  68.1 4.7 %stripes.1 = bf16[128,1024]{1,0:T(8,128)(2,1)} custom-call(s32[8,2]{1,0:T(8,128)S(1)} %copy.12.hub_ref, s32[1,128]{1,0:T(1,128)S(1)} %copy-done.1, s32[1,128]{1,0:T(1,128)S(1)} %copy-done.2, s32[1]{0:T(128)S(6)} %copy.14.live, bf16[8,768,128]{2,1,0:T(8,128)(2,1)} %all-to-all-done.own, bf16[8,768,128]{2,1,0:T(8,128)(2,1)} %collective-permute-done.other, ...), custom_call_target="tpu_custom_call" | custom-call | tf_op jit(solution)/shard_map/stripes/pallas_call | solution.py:177
  72.8 4.0 %all-to-all-start.1 = ((bf16[4,32,1024]{2,1,0:T(8,128)(2,1)}), bf16[4,32,1024]{2,1,0:T(8,128)(2,1)S(1)}, u32[]{:S(2)}, u32[]{:S(2)}) async-start(bf16[4,32,1024]{2,1,0:T(8,128)(2,1)} %bitcast.4), calls=%async_computation.1 | async-start | bytes 524288 | tf_op jit(solution)/shard_map/all_to_all | solution.py:203
  76.8 5.8 %all-to-all-done.1 = bf16[4,32,1024]{2,1,0:T(8,128)(2,1)S(1)} async-done(((bf16[4,32,1024]{2,1,0:T(8,128)(2,1)}), bf16[4,32,1024]{2,1,0:T(8,128)(2,1)S(1)}, u32[]{:S(2)}, u32[]{:S(2)}) %all-to-all-start.1) | async-done | bytes 262176 | tf_op jit(solution)/shard_map/all_to_all | solution.py:203
  82.6 0.0 copy-done
  82.6 0.9 %convolution_convert_fusion = bf16[1024,32]{0,1:T(8,128)(2,1)} fusion(bf16[128,1024]{1,0:T(8,128)(2,1)S(1)} %bitcast.5, bf16[128,128]{1,0:T(8,128)(2,1)S(1)} %copy-done, s32[]{:T(128)S(6)} %select_n.3), kind=kOutput, calls=%fused_computation | convolution fusion | flops 8421376 | bytes 360452 | tf_op jit(solution)/shard_map/dot_general | solution.py:205
Async XLA Ops:
  0.0 82.6 %copy-start = (bf16[128,128]{1,0:T(8,128)(2,1)S(1)}, bf16[128,128]{1,0:T(8,128)(2,1)}, u32[]{:S(2)}) copy-start(bf16[128,128]{1,0:T(8,128)(2,1)} %param.21) | copy-start | bytes 98308
  36.7 20.1 %all-to-all-start = ((bf16[8,768,128]{2,1,0:T(8,128)(2,1)}), bf16[8,768,128]{2,1,0:T(8,128)(2,1)}, u32[]{:S(2)}, u32[]{:S(2)}) async-start(bf16[8,768,128]{2,1,0:T(8,128)(2,1)} %select.1), calls=%async_computation | async-start | bytes 3145728 | tf_op jit(solution)/shard_map/all_to_all | solution.py:164
  41.4 23.4 %copy-start.3 = (s32[8,2]{0,1:T(2,128)S(1)}, s32[8,2]{0,1:T(2,128)}, u32[]{:S(2)}) copy-start(s32[8,2]{0,1:T(2,128)} %param.14) | copy-start | bytes 196
  41.4 26.7 %copy-start.1 = (s32[1,128]{1,0:T(1,128)S(1)}, s32[1,128]{1,0:T(1,128)}, u32[]{:S(2)}) copy-start(s32[1,128]{1,0:T(1,128)} %slot.1) | copy-start | bytes 1540
  41.4 26.7 %copy-start.2 = (s32[1,128]{1,0:T(1,128)S(1)}, s32[1,128]{1,0:T(1,128)}, u32[]{:S(2)}) copy-start(s32[1,128]{1,0:T(1,128)} %target.1) | copy-start | bytes 1540
  56.8 11.3 %collective-permute-start = (bf16[8,768,128]{2,1,0:T(8,128)(2,1)}, bf16[8,768,128]{2,1,0:T(8,128)(2,1)}, u32[]{:S(2)}, u32[]{:S(2)}) collective-permute-start(bf16[8,768,128]{2,1,0:T(8,128)(2,1)} %all-to-all-done.own), channel_id=1, source_target_pairs={{0,4},{4,0},{1,5},{5,1},{2,6},{6,2},{3,7},{7,3},{8,12},{12,8},{9,1... | collective-permute-start | bytes 4718600 | tf_op jit(solution)/shard_map/ppermute | solution.py:176
  72.8 9.8 %all-to-all-start.1 = ((bf16[4,32,1024]{2,1,0:T(8,128)(2,1)}), bf16[4,32,1024]{2,1,0:T(8,128)(2,1)S(1)}, u32[]{:S(2)}, u32[]{:S(2)}) async-start(bf16[4,32,1024]{2,1,0:T(8,128)(2,1)} %bitcast.4), calls=%async_computation.1 | async-start | bytes 524288 | tf_op jit(solution)/shard_map/all_to_all | solution.py:203

commit v6 on v5

--- a/solution.py
+++ b/solution.py
@@ -9,7 +9,7 @@
 ROWB, TILE, W = 8, 128, 32
 NEAR = Y * L
 CAP = 128
-EARLY = 96
+EARLY = 56
 BLOCKS = ROWB * W
 PAY = BLOCKS + 16
 SENT = (C + 1) * H * W
@@ -193,7 +193,7 @@
         stripe_slot,
         stripe_target,
         stripe_live,
-        in_hbm(received),
+        received,
         in_hbm(other),
         in_hbm(base),
         in_vmem(early),

time: 84 us -> 83.9 us (level)
  no operation moved by 1% of the time
where the time goes in v6:
time: 83.9 us; the launch traced here: 83.4 us
  blocking collectives  33.2 us (40%)
  waiting for transfers between devices  20.3 us (24%)
  starting transfers between devices  16.7 us (20%)
  Pallas kernels  10.8 us (13%)
  between operations  1.38 us (2%)
  matrix products  0.91 us (1%)
    all_gather x1, blocking collectives, local(): gathered = lax.all_gather(payload, 'h', axis=0, tiled=True)  33.2 us
    all_to_all x1, waiting for transfers between devices, local(): lax.all_to_all(outgoing, ('l', 'y'), split_axis=0, concat_axis=0, tiled=T...  12.1 us
    ppermute x1, starting transfers between devices, local(): other = lax.ppermute(received, 'c', [(0, 1), (1, 0)])  7.97 us
    all_to_all x1, waiting for transfers between devices, local(): lax.all_to_all(aggregated, 'x', split_axis=0, concat_axis=0, tiled=True)  5.81 us
    pallas_call x1, Pallas kernels, local(): pl.pallas_call(stripe_kernel, out_shape=pltpu.HBM((COL * W, ROWB * TILE),...  4.87 us
    all_to_all x1, starting transfers between devices, local(): lax.all_to_all(outgoing, ('l', 'y'), split_axis=0, concat_axis=0, tiled=T...  4.67 us
    all_to_all x1, starting transfers between devices, local(): lax.all_to_all(aggregated, 'x', split_axis=0, concat_axis=0, tiled=True)  4.02 us
    pallas_call x1, Pallas kernels, local(): pl.pallas_call(fetch_kernel, out_shape=(pltpu.HBM((BLOCKS, TILE), f32), p...  3.15 us
  transfers between devices with their start and end apart: 3, of which 3 were waited for; matrix products, arithmetic and copies ran while one was open for 0% of the time, Pallas kernels for 4%

profile of v6, /device:TPU:1, one launch (start us, length us, event | category | flops | bytes accessed | tf_op | source)
XLA Modules:
  0.0 83.4 jit_solution(18005145058869761656)
XLA Ops:
  0.0 0.0 copy-start
  0.7 0.9 %pack.1 = bf16[272,128]{1,0:T(8,128)(2,1)S(1)} custom-call(s32[1]{0:T(128)S(6)} %copy.13.hub_list, bf16[32,1024]{1,0:T(8,128)(2,1)} %bitcast.6, s32[1,128]{1,0:T(1,128)} %send.1), custom_call_target="tpu_custom_call" | custom-call | tf_op jit(solution)/shard_map/pack/pallas_call | solution.py:138
  1.5 33.2 %all_gather.3.gathered = bf16[2176,128]{1,0:T(8,128)(2,1)S(1)} all-gather(bf16[272,128]{1,0:T(8,128)(2,1)S(1)} %pack.1), channel_id=1, replica_groups=mesh['y'=4,'h'=8,'l'=2,'c'=2,'x'=4] {'h'}, dimensions={0}, use_global_device_ids=true | all-gather | bytes 626688 | tf_op jit(solution)/shard_map/all_gather | solution.py:146
  34.7 2.0 %select.1 = bf16[8,768,128]{2,1,0:T(8,128)(2,1)} custom-call(bf16[2176,128]{1,0:T(8,128)(2,1)S(1)} %all_gather.3.gathered), custom_call_target="tpu_custom_call" | custom-call | bytes 6000000 | tf_op jit(solution)/shard_map/select/pallas_call | solution.py:147
  36.7 4.7 %all-to-all-start = ((bf16[8,768,128]{2,1,0:T(8,128)(2,1)}), bf16[8,768,128]{2,1,0:T(8,128)(2,1)S(1)}, u32[]{:S(2)}, u32[]{:S(2)}) async-start(bf16[8,768,128]{2,1,0:T(8,128)(2,1)} %select.1), calls=%async_computation | async-start | bytes 3145728 | tf_op jit(solution)/shard_map/all_to_all | solution.py:164
  41.4 0.0 copy-start.3
  41.4 0.0 copy-start.1
  41.4 0.0 copy-start.2
  41.4 3.2 %fetch.1 = (f32[256,128]{1,0:T(8,128)}, bf16[56,128,128]{2,1,0:T(8,128)(2,1)S(1)}) custom-call(bf16[32,1024]{1,0:T(8,128)(2,1)} %bitcast.7, bf16[8,128,128]{2,1,0:T(8,128)(2,1)} %local_tiles.1, bf16[128,128,128]{2,1,0:T(8,128)(2,1)} %tiles_hbm.3), custom_call_target="tpu_custom_call" | custom-call | flops 8400000 | bytes 3000000 | tf_op jit(solution)/shard_map/fetch/pallas_call | solution.py:165
  44.6 12.1 %all-to-all-done.own = bf16[8,768,128]{2,1,0:T(8,128)(2,1)S(1)} async-done(((bf16[8,768,128]{2,1,0:T(8,128)(2,1)}), bf16[8,768,128]{2,1,0:T(8,128)(2,1)S(1)}, u32[]{:S(2)}, u32[]{:S(2)}) %all-to-all-start) | async-done | bytes 1572896 | tf_op jit(solution)/shard_map/all_to_all | solution.py:164
  56.7 8.0 %collective-permute-start = (bf16[8,768,128]{2,1,0:T(8,128)(2,1)S(1)}, bf16[8,768,128]{2,1,0:T(8,128)(2,1)}, u32[]{:S(2)}, u32[]{:S(2)}) collective-permute-start(bf16[8,768,128]{2,1,0:T(8,128)(2,1)S(1)} %all-to-all-done.own), channel_id=1, source_target_pairs={{0,4},{4,0},{1,5},{5,1},{2,6},{6,2},{3,7},{7,3},{8,12},{12,8},{9,1... | collective-permute-start | bytes 4718600 | tf_op jit(solution)/shard_map/ppermute | solution.py:176
  64.6 0.0 copy-done.3
  64.7 0.1 copy.12.hub_ref
  65.4 2.4 %collective-permute-done.other = bf16[8,768,128]{2,1,0:T(8,128)(2,1)} collective-permute-done((bf16[8,768,128]{2,1,0:T(8,128)(2,1)S(1)}, bf16[8,768,128]{2,1,0:T(8,128)(2,1)}, u32[]{:S(2)}, u32[]{:S(2)}) %collective-permute-start) | collective-permute-done | bytes 1572896 | tf_op jit(solution)/shard_map/ppermute | solution.py:176
  67.8 0.0 copy-done.1
  67.8 0.0 copy-done.2
  67.8 4.9 %stripes.1 = bf16[128,1024]{1,0:T(8,128)(2,1)} custom-call(s32[8,2]{1,0:T(8,128)S(1)} %copy.12.hub_ref, s32[1,128]{1,0:T(1,128)S(1)} %copy-done.1, s32[1,128]{1,0:T(1,128)S(1)} %copy-done.2, s32[1]{0:T(128)S(6)} %copy.14.live, bf16[8,768,128]{2,1,0:T(8,128)(2,1)S(1)} %all-to-all-done.own, bf16[8,768,128]{2,1,0:T(8,128)(2,1)} %collective-permute-done.other, ...), custom_call_target="tpu_custom_call" | custom-call | tf_op jit(solution)/shard_map/stripes/pallas_call | solution.py:177
  72.7 4.0 %all-to-all-start.1 = ((bf16[4,32,1024]{2,1,0:T(8,128)(2,1)}), bf16[4,32,1024]{2,1,0:T(8,128)(2,1)S(1)}, u32[]{:S(2)}, u32[]{:S(2)}) async-start(bf16[4,32,1024]{2,1,0:T(8,128)(2,1)} %bitcast.4), calls=%async_computation.1 | async-start | bytes 524288 | tf_op jit(solution)/shard_map/all_to_all | solution.py:203
  76.7 5.8 %all-to-all-done.1 = bf16[4,32,1024]{2,1,0:T(8,128)(2,1)S(1)} async-done(((bf16[4,32,1024]{2,1,0:T(8,128)(2,1)}), bf16[4,32,1024]{2,1,0:T(8,128)(2,1)S(1)}, u32[]{:S(2)}, u32[]{:S(2)}) %all-to-all-start.1) | async-done | bytes 262176 | tf_op jit(solution)/shard_map/all_to_all | solution.py:203
  82.5 0.0 copy-done
  82.5 0.9 %convolution_convert_fusion = bf16[1024,32]{0,1:T(8,128)(2,1)} fusion(bf16[128,1024]{1,0:T(8,128)(2,1)S(1)} %bitcast.5, bf16[128,128]{1,0:T(8,128)(2,1)S(1)} %copy-done, s32[]{:T(128)S(6)} %select_n.3), kind=kOutput, calls=%fused_computation | convolution fusion | flops 8421376 | bytes 360452 | tf_op jit(solution)/shard_map/dot_general | solution.py:205
Async XLA Ops:
  0.0 82.5 %copy-start = (bf16[128,128]{1,0:T(8,128)(2,1)S(1)}, bf16[128,128]{1,0:T(8,128)(2,1)}, u32[]{:S(2)}) copy-start(bf16[128,128]{1,0:T(8,128)(2,1)} %param.21) | copy-start | bytes 98308
  36.7 20.0 %all-to-all-start = ((bf16[8,768,128]{2,1,0:T(8,128)(2,1)}), bf16[8,768,128]{2,1,0:T(8,128)(2,1)S(1)}, u32[]{:S(2)}, u32[]{:S(2)}) async-start(bf16[8,768,128]{2,1,0:T(8,128)(2,1)} %select.1), calls=%async_computation | async-start | bytes 3145728 | tf_op jit(solution)/shard_map/all_to_all | solution.py:164
  41.4 23.3 %copy-start.3 = (s32[8,2]{0,1:T(2,128)S(1)}, s32[8,2]{0,1:T(2,128)}, u32[]{:S(2)}) copy-start(s32[8,2]{0,1:T(2,128)} %param.14) | copy-start | bytes 196
  41.4 26.4 %copy-start.1 = (s32[1,128]{1,0:T(1,128)S(1)}, s32[1,128]{1,0:T(1,128)}, u32[]{:S(2)}) copy-start(s32[1,128]{1,0:T(1,128)} %slot.1) | copy-start | bytes 1540
  41.4 26.4 %copy-start.2 = (s32[1,128]{1,0:T(1,128)S(1)}, s32[1,128]{1,0:T(1,128)}, u32[]{:S(2)}) copy-start(s32[1,128]{1,0:T(1,128)} %target.1) | copy-start | bytes 1540
  56.7 11.1 %collective-permute-start = (bf16[8,768,128]{2,1,0:T(8,128)(2,1)S(1)}, bf16[8,768,128]{2,1,0:T(8,128)(2,1)}, u32[]{:S(2)}, u32[]{:S(2)}) collective-permute-start(bf16[8,768,128]{2,1,0:T(8,128)(2,1)S(1)} %all-to-all-done.own), channel_id=1, source_target_pairs={{0,4},{4,0},{1,5},{5,1},{2,6},{6,2},{3,7},{7,3},{8,12},{12,8},{9,1... | collective-permute-start | bytes 4718600 | tf_op jit(solution)/shard_map/ppermute | solution.py:176
  72.7 9.8 %all-to-all-start.1 = ((bf16[4,32,1024]{2,1,0:T(8,128)(2,1)}), bf16[4,32,1024]{2,1,0:T(8,128)(2,1)S(1)}, u32[]{:S(2)}, u32[]{:S(2)}) async-start(bf16[4,32,1024]{2,1,0:T(8,128)(2,1)} %bitcast.4), calls=%async_computation.1 | async-start | bytes 524288 | tf_op jit(solution)/shard_map/all_to_all | solution.py:203

commit v7 on v5

--- a/solution.py
+++ b/solution.py
@@ -9,7 +9,7 @@
 ROWB, TILE, W = 8, 128, 32
 NEAR = Y * L
 CAP = 128
-EARLY = 96
+EARLY = 104
 BLOCKS = ROWB * W
 PAY = BLOCKS + 16
 SENT = (C + 1) * H * W

time: 84 us -> 84 us (level)
  no operation moved by 1% of the time
where the time goes in v7:
time: 84 us; the launch traced here: 83.6 us
  blocking collectives  33.2 us (40%)
  waiting for transfers between devices  20.2 us (24%)
  starting transfers between devices  16.7 us (20%)
  Pallas kernels  11.1 us (13%)
  between operations  1.38 us (2%)
  matrix products  0.91 us (1%)
    all_gather x1, blocking collectives, local(): gathered = lax.all_gather(payload, 'h', axis=0, tiled=True)  33.2 us
    all_to_all x1, waiting for transfers between devices, local(): lax.all_to_all(outgoing, ('l', 'y'), split_axis=0, concat_axis=0, tiled=T...  11.8 us
    ppermute x1, starting transfers between devices, local(): other = lax.ppermute(received, 'c', [(0, 1), (1, 0)])  7.97 us
    all_to_all x1, waiting for transfers between devices, local(): lax.all_to_all(aggregated, 'x', split_axis=0, concat_axis=0, tiled=True)  5.81 us
    pallas_call x1, Pallas kernels, local(): pl.pallas_call(stripe_kernel, out_shape=pltpu.HBM((COL * W, ROWB * TILE),...  4.69 us
    all_to_all x1, starting transfers between devices, local(): lax.all_to_all(outgoing, ('l', 'y'), split_axis=0, concat_axis=0, tiled=T...  4.67 us
    all_to_all x1, starting transfers between devices, local(): lax.all_to_all(aggregated, 'x', split_axis=0, concat_axis=0, tiled=True)  4.03 us
    pallas_call x1, Pallas kernels, local(): pl.pallas_call(fetch_kernel, out_shape=(pltpu.HBM((BLOCKS, TILE), f32), p...  3.61 us
  transfers between devices with their start and end apart: 3, of which 3 were waited for; matrix products, arithmetic and copies ran while one was open for 0% of the time, Pallas kernels for 4%

profile of v7, /device:TPU:1, one launch (start us, length us, event | category | flops | bytes accessed | tf_op | source)
XLA Modules:
  0.0 83.6 jit_solution(1400501321233955227)
XLA Ops:
  0.0 0.0 copy-start
  0.7 0.9 %pack.1 = bf16[272,128]{1,0:T(8,128)(2,1)S(1)} custom-call(s32[1]{0:T(128)S(6)} %copy.13.hub_list, bf16[32,1024]{1,0:T(8,128)(2,1)} %bitcast.6, s32[1,128]{1,0:T(1,128)} %send.1), custom_call_target="tpu_custom_call" | custom-call | tf_op jit(solution)/shard_map/pack/pallas_call | solution.py:138
  1.5 33.2 %all_gather.3.gathered = bf16[2176,128]{1,0:T(8,128)(2,1)S(1)} all-gather(bf16[272,128]{1,0:T(8,128)(2,1)S(1)} %pack.1), channel_id=1, replica_groups=mesh['y'=4,'h'=8,'l'=2,'c'=2,'x'=4] {'h'}, dimensions={0}, use_global_device_ids=true | all-gather | bytes 626688 | tf_op jit(solution)/shard_map/all_gather | solution.py:146
  34.7 2.0 %select.1 = bf16[8,768,128]{2,1,0:T(8,128)(2,1)} custom-call(bf16[2176,128]{1,0:T(8,128)(2,1)S(1)} %all_gather.3.gathered), custom_call_target="tpu_custom_call" | custom-call | bytes 6000000 | tf_op jit(solution)/shard_map/select/pallas_call | solution.py:147
  36.7 4.7 %all-to-all-start = ((bf16[8,768,128]{2,1,0:T(8,128)(2,1)}), bf16[8,768,128]{2,1,0:T(8,128)(2,1)}, u32[]{:S(2)}, u32[]{:S(2)}) async-start(bf16[8,768,128]{2,1,0:T(8,128)(2,1)} %select.1), calls=%async_computation | async-start | bytes 3145728 | tf_op jit(solution)/shard_map/all_to_all | solution.py:164
  41.4 0.0 copy-start.3
  41.4 0.0 copy-start.1
  41.4 0.0 copy-start.2
  41.4 3.6 %fetch.1 = (f32[256,128]{1,0:T(8,128)}, bf16[104,128,128]{2,1,0:T(8,128)(2,1)S(1)}) custom-call(bf16[32,1024]{1,0:T(8,128)(2,1)} %bitcast.7, bf16[8,128,128]{2,1,0:T(8,128)(2,1)} %local_tiles.1, bf16[128,128,128]{2,1,0:T(8,128)(2,1)} %tiles_hbm.3), custom_call_target="tpu_custom_call" | custom-call | flops 8400000 | bytes 3000000 | tf_op jit(solution)/shard_map/fetch/pallas_call | solution.py:165
  45.0 11.8 %all-to-all-done.own = bf16[8,768,128]{2,1,0:T(8,128)(2,1)} async-done(((bf16[8,768,128]{2,1,0:T(8,128)(2,1)}), bf16[8,768,128]{2,1,0:T(8,128)(2,1)}, u32[]{:S(2)}, u32[]{:S(2)}) %all-to-all-start) | async-done | bytes 1572896 | tf_op jit(solution)/shard_map/all_to_all | solution.py:164
  56.8 8.0 %collective-permute-start = (bf16[8,768,128]{2,1,0:T(8,128)(2,1)}, bf16[8,768,128]{2,1,0:T(8,128)(2,1)}, u32[]{:S(2)}, u32[]{:S(2)}) collective-permute-start(bf16[8,768,128]{2,1,0:T(8,128)(2,1)} %all-to-all-done.own), channel_id=1, source_target_pairs={{0,4},{4,0},{1,5},{5,1},{2,6},{6,2},{3,7},{7,3},{8,12},{12,8},{9,1... | collective-permute-start | bytes 4718600 | tf_op jit(solution)/shard_map/ppermute | solution.py:176
  64.7 0.0 copy-done.3
  64.8 0.1 copy.12.hub_ref
  65.5 2.6 %collective-permute-done.other = bf16[8,768,128]{2,1,0:T(8,128)(2,1)} collective-permute-done((bf16[8,768,128]{2,1,0:T(8,128)(2,1)}, bf16[8,768,128]{2,1,0:T(8,128)(2,1)}, u32[]{:S(2)}, u32[]{:S(2)}) %collective-permute-start) | collective-permute-done | bytes 1572896 | tf_op jit(solution)/shard_map/ppermute | solution.py:176
  68.1 0.0 copy-done.1
  68.1 0.0 copy-done.2
  68.1 4.7 %stripes.1 = bf16[128,1024]{1,0:T(8,128)(2,1)} custom-call(s32[8,2]{1,0:T(8,128)S(1)} %copy.12.hub_ref, s32[1,128]{1,0:T(1,128)S(1)} %copy-done.1, s32[1,128]{1,0:T(1,128)S(1)} %copy-done.2, s32[1]{0:T(128)S(6)} %copy.14.live, bf16[8,768,128]{2,1,0:T(8,128)(2,1)} %all-to-all-done.own, bf16[8,768,128]{2,1,0:T(8,128)(2,1)} %collective-permute-done.other, ...), custom_call_target="tpu_custom_call" | custom-call | tf_op jit(solution)/shard_map/stripes/pallas_call | solution.py:177
  72.8 4.0 %all-to-all-start.1 = ((bf16[4,32,1024]{2,1,0:T(8,128)(2,1)}), bf16[4,32,1024]{2,1,0:T(8,128)(2,1)S(1)}, u32[]{:S(2)}, u32[]{:S(2)}) async-start(bf16[4,32,1024]{2,1,0:T(8,128)(2,1)} %bitcast.4), calls=%async_computation.1 | async-start | bytes 524288 | tf_op jit(solution)/shard_map/all_to_all | solution.py:203
  76.8 5.8 %all-to-all-done.1 = bf16[4,32,1024]{2,1,0:T(8,128)(2,1)S(1)} async-done(((bf16[4,32,1024]{2,1,0:T(8,128)(2,1)}), bf16[4,32,1024]{2,1,0:T(8,128)(2,1)S(1)}, u32[]{:S(2)}, u32[]{:S(2)}) %all-to-all-start.1) | async-done | bytes 262176 | tf_op jit(solution)/shard_map/all_to_all | solution.py:203
  82.6 0.0 copy-done
  82.6 0.9 %convolution_convert_fusion = bf16[1024,32]{0,1:T(8,128)(2,1)} fusion(bf16[128,1024]{1,0:T(8,128)(2,1)S(1)} %bitcast.5, bf16[128,128]{1,0:T(8,128)(2,1)S(1)} %copy-done, s32[]{:T(128)S(6)} %select_n.3), kind=kOutput, calls=%fused_computation | convolution fusion | flops 8421376 | bytes 360452 | tf_op jit(solution)/shard_map/dot_general | solution.py:205
Async XLA Ops:
  0.0 82.6 %copy-start = (bf16[128,128]{1,0:T(8,128)(2,1)S(1)}, bf16[128,128]{1,0:T(8,128)(2,1)}, u32[]{:S(2)}) copy-start(bf16[128,128]{1,0:T(8,128)(2,1)} %param.21) | copy-start | bytes 98308
  36.7 20.1 %all-to-all-start = ((bf16[8,768,128]{2,1,0:T(8,128)(2,1)}), bf16[8,768,128]{2,1,0:T(8,128)(2,1)}, u32[]{:S(2)}, u32[]{:S(2)}) async-start(bf16[8,768,128]{2,1,0:T(8,128)(2,1)} %select.1), calls=%async_computation | async-start | bytes 3145728 | tf_op jit(solution)/shard_map/all_to_all | solution.py:164
  41.4 23.4 %copy-start.3 = (s32[8,2]{0,1:T(2,128)S(1)}, s32[8,2]{0,1:T(2,128)}, u32[]{:S(2)}) copy-start(s32[8,2]{0,1:T(2,128)} %param.14) | copy-start | bytes 196
  41.4 26.7 %copy-start.1 = (s32[1,128]{1,0:T(1,128)S(1)}, s32[1,128]{1,0:T(1,128)}, u32[]{:S(2)}) copy-start(s32[1,128]{1,0:T(1,128)} %slot.1) | copy-start | bytes 1540
  41.4 26.7 %copy-start.2 = (s32[1,128]{1,0:T(1,128)S(1)}, s32[1,128]{1,0:T(1,128)}, u32[]{:S(2)}) copy-start(s32[1,128]{1,0:T(1,128)} %target.1) | copy-start | bytes 1540
  56.8 11.3 %collective-permute-start = (bf16[8,768,128]{2,1,0:T(8,128)(2,1)}, bf16[8,768,128]{2,1,0:T(8,128)(2,1)}, u32[]{:S(2)}, u32[]{:S(2)}) collective-permute-start(bf16[8,768,128]{2,1,0:T(8,128)(2,1)} %all-to-all-done.own), channel_id=1, source_target_pairs={{0,4},{4,0},{1,5},{5,1},{2,6},{6,2},{3,7},{7,3},{8,12},{12,8},{9,1... | collective-permute-start | bytes 4718600 | tf_op jit(solution)/shard_map/ppermute | solution.py:176
  72.8 9.8 %all-to-all-start.1 = ((bf16[4,32,1024]{2,1,0:T(8,128)(2,1)}), bf16[4,32,1024]{2,1,0:T(8,128)(2,1)S(1)}, u32[]{:S(2)}, u32[]{:S(2)}) async-start(bf16[4,32,1024]{2,1,0:T(8,128)(2,1)} %bitcast.4), calls=%async_computation.1 | async-start | bytes 524288 | tf_op jit(solution)/shard_map/all_to_all | solution.py:203
